TPU v7x, 32 devices: a whole 2x2x4 slice. The times are simulated.
32 devices in a mesh: gz: 4 (over y, core), xy: 8 (over z, x).
Axes of the slice: x: 2, y: 2, z: 4, core: 2. Of those that a mesh axis runs over, the one named last changes fastest.
Arguments:
- density: float32 [128, 256, 1024], P('gz', 'xy')
- uptake: float32 [128, 256, 1024], P('gz', 'xy'), may hold values from 0.5 to 50
- brick_values: bfloat16 [2304, 4096], P(('gz', 'xy'))
- brick_ids: int32 [2304], P(('gz', 'xy')), may hold values from 0 to 8191, as said below
- slot_counts: int32 [32, 9], P(('gz', 'xy')), may hold values from 0 to 8, as said below
Outputs:
- supply: float32 [128, 256, 1024], P('gz', 'xy')
- concentration: float32 [128, 256, 1024], P('gz', 'xy')
Inputs may be any that keep to these rules, and one draw needn't show every extreme that they name: `brick_ids`: the slots 8 j to 8 j + 7 of each device (j = 0 to 8) name bricks of the device whose gz index differs by j // 3 - 1 and whose xy index differs by j % 3 - 1, or of the device itself where no such device exists; the first and the last brick of the grid are both named. `slot_counts`: entry j of a device counts the live slots at the start of its block j; it is 0 where block j's device does not exist, and 8 for j = 4.
All inputs are finite; a program needn't handle non-finite values.
Results may differ from a plain program's by a relative error of at most 0.0014.
Values may be sent and summed in bfloat16 or wider, within the bound.
No kernel may reach another device: no remote copies, remote signals or barrier semaphores. Data moves between devices by JAX's collectives and lax.ppermute only.
A program may use at most 576 MiB of HBM per device.

v0:
```python
import jax
import jax.numpy as jnp
from jax import lax
from jax.sharding import PartitionSpec as P

EDGE = 16
CAP = 8
LEVELS = 4
NU = 2
NC = 4
BRICK = 4096
SLOTS = 72


KAPPA = 32.0
OMEGA = 0.8


def extended(shard, sides, width):
    for axis, dim in sides:
        count, length = (lax.axis_size(axis), shard.shape[dim])
        up = [(i, (i + 1) % count) for i in range(count - 1)]
        down = [(j, i) for i, j in up]
        last = lax.slice_in_dim(shard, length - width, length, axis=dim)
        initial = lax.slice_in_dim(shard, 0, width, axis=dim)
        before = lax.ppermute(last, axis, up)
        after = lax.ppermute(initial, axis, down)
        shard = jnp.concatenate([before, shard, after], axis=dim)
    return shard


def from_behind(block, axis, distance):
    devices = range(lax.axis_size(axis))
    route = [(i - distance, i) for i in devices if i - distance in devices]
    return lax.ppermute(block, axis, route)


def as_sent(shard):
    return jax.tree.map(lambda a: a.astype(jnp.bfloat16) if a.dtype == jnp.float32 else a, shard)


def neighbours(padded, values):
    y_padded = jnp.pad(values, ((0, 0), (0, 0), (1, 1)))
    summed = padded[2:, 1:-1] + padded[:-2, 1:-1]
    summed = summed + padded[1:-1, 2:] + padded[1:-1, :-2]
    summed = summed + y_padded[:, :, 2:] + y_padded[:, :, :-2]
    return summed


def operate(values, diagonal, spread):
    padded = extended(values, (("gz", 0), ("xy", 1)), 1)
    return diagonal * values - spread * neighbours(padded, values)


def smooth_once(values, source, diagonal, spread):
    return values + OMEGA * (source - operate(values, diagonal, spread)) / diagonal


def shrink(values):
    zsize, xsize, ysize = values.shape
    return values.reshape(zsize // 2, 2, xsize // 2, 2, ysize // 2, 2).mean(axis=(1, 3, 5))


def expand(values):
    return jnp.repeat(jnp.repeat(jnp.repeat(values, 2, 0), 2, 1), 2, 2)


def descend(level_index, source, start, rates):
    spread = KAPPA / 4.0**level_index
    diagonal = 1.0 + rates + 6.0 * spread
    estimate = start
    if level_index == LEVELS - 1:
        for repeat in range(NC):
            estimate = smooth_once(estimate, source, diagonal, spread)
        return estimate
    for repeat in range(NU):
        estimate = smooth_once(estimate, source, diagonal, spread)
    remainder = source - operate(estimate, diagonal, spread)
    coarser = shrink(remainder)
    update = descend(level_index + 1, coarser, jnp.zeros_like(coarser), shrink(rates))
    estimate = estimate + expand(update)
    for repeat in range(NU):
        estimate = smooth_once(estimate, source, diagonal, spread)
    return estimate


def slab_step(labels, payload, offset):
    return from_behind((labels, payload), "gz", offset)


def tile_step(labels, payload, offset):
    return (
        from_behind(as_sent(labels), "xy", offset).astype(labels.dtype),
        from_behind(payload, "xy", offset),
    )


def shards(density, uptake, brick_values, brick_ids, slot_counts):
    depth_z, width_x, length_y = density.shape
    per_z = depth_z // EDGE
    per_x = width_x // EDGE
    per_y = length_y // EDGE
    tiles = lax.axis_size("xy")
    bricks_x = per_x * tiles
    within = jnp.arange(SLOTS, dtype=jnp.int32)
    is_live = within % CAP < slot_counts[0, within // CAP]
    masked = jnp.where(is_live[:, None], brick_values, jnp.zeros_like(brick_values))
    value_grid = masked.reshape(3, 3, CAP, BRICK)
    label_grid = brick_ids.reshape(3, 3, CAP)
    first_hop = {}
    for offset in (1, -1):
        first_hop[offset] = slab_step(label_grid[offset + 1], value_grid[offset + 1], offset)
    held_ids = jnp.concatenate([label_grid[1], first_hop[1][0], first_hop[-1][0]], axis=1)
    held_values = jnp.concatenate([value_grid[1], first_hop[1][1], first_hop[-1][1]], axis=1)
    second_hop = {}
    for offset in (1, -1):
        second_hop[offset] = tile_step(held_ids[offset + 1], held_values[offset + 1], offset)
    arrived_ids = jnp.concatenate([held_ids[1], second_hop[1][0], second_hop[-1][0]], axis=0)
    arrived = jnp.concatenate([held_values[1], second_hop[1][1], second_hop[-1][1]], axis=0)
    brick_y = arrived_ids % per_y
    rest_ids = arrived_ids // per_y
    brick_x = rest_ids % bricks_x
    brick_z = rest_ids // bricks_x
    local_brick = (brick_z % per_z * per_x + brick_x % per_x) * per_y + brick_y
    one_hot = (
        local_brick[None, :] == jnp.arange(per_z * per_x * per_y, dtype=jnp.int32)[:, None]
    ).astype(jnp.bfloat16)
    gathered = jnp.dot(one_hot, arrived, preferred_element_type=jnp.float32)
    secretion = (
        gathered.reshape(per_z, per_x, per_y, EDGE, EDGE, EDGE)
        .transpose(0, 3, 1, 4, 2, 5)
        .reshape(depth_z, width_x, length_y)
    )
    supply = density + secretion
    concentration = descend(0, supply, density, uptake)
    return (supply, concentration)


def solution(mesh):
    return jax.shard_map(
        shards,
        mesh=mesh,
        in_specs=(
            P("gz", "xy", None),
            P("gz", "xy", None),
            P(("gz", "xy"), None),
            P(("gz", "xy")),
            P(("gz", "xy"), None),
        ),
        out_specs=(P("gz", "xy", None), P("gz", "xy", None)),
        check_vma=False,
    )
```

profile of v0, /device:TPU:0, one launch (start us, length us, event | category | flops | bytes accessed | tf_op | source)
XLA Modules:
  0.0 1346.6 jit_solution(2080747353575344819)
XLA Ops:
  51.2 9.3 reshape.351
  60.5 24.0 %copy.99 = f32[2,16,2,16,64,16]{5,4,3,2,1,0:T(8,128)} copy(f32[2,16,2,16,64,16]{4,2,0,5,3,1:T(2,128)} %bitcast.37) | data formatting | bytes 8388608 | tf_op jit(solution)/shard_map/transpose | solution.py:131
  84.5 28.3 %reshape.352 = f32[32,32,1024]{2,1,0:T(8,128)} reshape(f32[2,16,2,16,64,16]{5,4,3,2,1,0:T(8,128)} %copy.99) | data formatting | bytes 8388608 | tf_op jit(solution)/shard_map/reshape | solution.py:132
  112.8 17.3 %fusion.7 = (f32[32,32,1024]{2,1,0:T(8,128)}, f32[32,32,1024]{2,1,0:T(8,128)S(1)}) fusion(f32[32,32,1024]{2,1,0:T(8,128)} %param.5, f32[34,32,1024]{2,1,0:T(8,128)} %copy-done.8, f32[34,1,1024]{2,1,0:T(1,128)S(1)} %collective-permute-done.11, f32[34,1,1024]{2,1,0:T(1,128)S(1)} %collective-permute-done.10, f32[1,32,1024]{2,1,0:T(8,128)S(1)} %collective-permute-done.9, ...), kind=kLoop, calls=%fused_computation.18 | loop fusion | flops 18874368 | bytes 25968640 | tf_op jit(solution)/shard_map/add | solution.py:56
  140.3 5.6 collective-permute-start.15
  151.3 18.8 %fusion.15 = f32[32,32,1024]{2,1,0:T(8,128)} fusion(f32[32,32,1024]{2,1,0:T(8,128)} %get-tuple-element.2, f32[32,32,1024]{2,1,0:T(8,128)S(1)} %get-tuple-element.3, f32[34,1,1024]{2,1,0:T(1,128)S(1)} %collective-permute-done.15, f32[1,32,1024]{2,1,0:T(8,128)S(1)} %collective-permute-done.12, f32[1,32,1024]{2,1,0:T(8,128)S(1)} %collective-permute-done.13, ...), kind=kLoop, calls=%fused_computation.26 | loop fusion | flops 22020096 | bytes 17317888 | tf_op jit(solution)/shard_map/add | solution.py:56
  192.0 270.4 %reshape.354 = f32[16,2,16,2,512,2]{5,4,3,2,1,0:T(8,128)} reshape(f32[32,32,1024]{2,1,0:T(8,128)} %param.6) | data formatting | bytes 8388608 | tf_op jit(solution)/shard_map/reshape | solution.py:61
  462.3 81.0 %reduce_sum.55 = f32[16,16,512]{2,1,0:T(8,128)} reduce(f32[16,2,16,2,512,2]{5,4,3,2,1,0:T(8,128)} %reshape.354, f32[]{:T(128)} %constant.132.clone.1), dimensions={1,3,5}, to_apply=%region_1.2 | reduce | flops 917504 | bytes 4718596 | tf_op jit(solution)/shard_map/reduce_sum | solution.py:61
  547.0 5.8 collective-permute-start.23
  552.9 21.3 %fusion.20 = f32[32,32,1024]{2,1,0:T(8,128)} fusion(f32[32,32,1024]{2,1,0:T(8,128)} %copy-done.4, f32[32,32,1024]{2,1,0:T(8,128)} %fusion.15, f32[34,1,1024]{2,1,0:T(1,128)} %collective-permute-done.19, f32[1,32,1024]{2,1,0:T(8,128)S(1)} %copy-done.12, f32[1,32,1024]{2,1,0:T(8,128)S(1)} %copy-done.14, f32[34,1,1024]{2,1,0:T(1,128)} %collective-permute-done.18, ...), kind=kLoop, calls=%fused_computation.31 | loop fusion | flops 18874368 | bytes 17317888 | tf_op jit(solution)/shard_map/sub | solution.py:78
  574.2 270.4 %reshape.353 = f32[16,2,16,2,512,2]{5,4,3,2,1,0:T(8,128)} reshape(f32[32,32,1024]{2,1,0:T(8,128)} %fusion.20) | data formatting | bytes 8388608 | tf_op jit(solution)/shard_map/reshape | solution.py:61
  844.5 80.2 %reduce_sum.54 = f32[16,16,512]{2,1,0:T(8,128)S(1)} reduce(f32[16,2,16,2,512,2]{5,4,3,2,1,0:T(8,128)} %reshape.353, f32[]{:T(128)} %constant.132.clone.1), dimensions={1,3,5}, to_apply=%region_0.1 | reduce | flops 917504 | bytes 4718596 | tf_op jit(solution)/shard_map/reduce_sum | solution.py:61
  945.7 5.7 collective-permute-start.33
  959.7 5.8 collective-permute-start.35
  965.9 34.9 %reshape.355 = f32[8,2,8,2,256,2]{5,4,3,2,1,0:T(8,128)} reshape(f32[16,16,512]{2,1,0:T(8,128)S(1)} %get-tuple-element.45) | data formatting | bytes 1048576 | tf_op jit(solution)/shard_map/reshape | solution.py:61
  1000.8 12.2 reduce_sum.56
  1013.0 34.9 %div.115 = f32[8,2,8,2,256,2]{5,4,3,2,1,0:T(8,128)} reshape(f32[16,16,512]{2,1,0:T(8,128)S(1)} %get-tuple-element.44) | data formatting | bytes 1048576 | tf_op jit(solution)/shard_map/div | solution.py:61
  1047.9 12.2 reduce_sum.57
  1080.0 5.7 collective-permute-start.45
  1093.9 5.9 collective-permute-start.47
  1151.6 5.7 collective-permute-start.59
  1167.6 5.7 collective-permute-start.63
  1183.0 5.7 collective-permute-start.67
  1208.1 5.7 collective-permute-start.71
  1224.4 6.0 collective-permute-start.75
  1234.0 7.7 copy.107
  1241.7 11.8 broadcast_in_dim.65
  1253.6 11.4 copy.108
  1279.0 5.8 collective-permute-start.79
  1287.8 18.8 %fusion.28 = f32[32,32,1024]{2,1,0:T(8,128)} fusion(f32[32,32,1024]{2,1,0:T(8,128)} %copy-done.6, f32[32,32,1024]{2,1,0:T(8,128)S(1)} %copy-done.5, f32[34,1,1024]{2,1,0:T(1,128)S(1)} %collective-permute-done.79, f32[1,32,1024]{2,1,0:T(8,128)S(1)} %collective-permute-done.76, f32[1,32,1024]{2,1,0:T(8,128)S(1)} %collective-permute-done.77, ...), kind=kLoop, calls=%fused_computation.39 | loop fusion | flops 22020096 | bytes 17317888 | tf_op jit(solution)/shard_map/add | solution.py:56
  1308.9 6.4 collective-permute-start.81
  1327.2 18.9 %fusion.36 = f32[32,32,1024]{2,1,0:T(8,128)} fusion(f32[32,32,1024]{2,1,0:T(8,128)} %fusion.28, f32[32,32,1024]{2,1,0:T(8,128)S(1)} %copy-done.5, f32[34,1,1024]{2,1,0:T(1,128)S(1)} %collective-permute-done.83, f32[1,32,1024]{2,1,0:T(8,128)S(1)} %collective-permute-done.80, f32[1,32,1024]{2,1,0:T(8,128)S(1)} %collective-permute-done.81, ...), kind=kLoop, calls=%fused_computation.47 | loop fusion | flops 22020096 | bytes 17317888 | tf_op jit(solution)/shard_map/add | solution.py:56
  (282 shorter events, 284.6 us)
Async XLA Ops:
  1.6 18.3 %collective-permute-start = (s32[3,8]{1,0:T(4,128)S(1)}, s32[3,8]{1,0:T(4,128)S(1)}, u32[]{:S(2)}, u32[]{:S(2)}) collective-permute-start(s32[3,8]{1,0:T(4,128)S(1)} %squeeze.35), channel_id=1, source_target_pairs={{0,8},{8,16},{16,24},{1,9},{9,17},{17,25},{2,10},{10,18},{18,26},{... | collective-permute-start | bytes 296 | tf_op jit(solution)/shard_map/ppermute | solution.py:35
  4.0 15.9 %collective-permute-start.1 = (s32[3,8]{1,0:T(4,128)S(1)}, s32[3,8]{1,0:T(4,128)S(1)}, u32[]{:S(2)}, u32[]{:S(2)}) collective-permute-start(s32[3,8]{1,0:T(4,128)S(1)} %squeeze.36), channel_id=1, source_target_pairs={{8,0},{16,8},{24,16},{9,1},{17,9},{25,17},{10,2},{18,10},{26,18},{... | collective-permute-start | bytes 296 | tf_op jit(solution)/shard_map/ppermute | solution.py:35
  8.1 23.4 %collective-permute-start.4 = (bf16[3,8,4096]{2,1,0:T(8,128)(2,1)S(1)}, bf16[3,8,4096]{2,1,0:T(8,128)(2,1)S(1)}, u32[]{:S(2)}, u32[]{:S(2)}) collective-permute-start(bf16[3,8,4096]{2,1,0:T(8,128)(2,1)S(1)} %get-tuple-element.39), channel_id=1, source_target_pairs={{0,8},{8,16},{16,24},{1,9},{9,17},{17,25},{2,10},{10,18},{18,26},{... | collective-permute-start | bytes 589832 | tf_op jit(solution)/shard_map/ppermute | solution.py:35
  13.3 18.3 %collective-permute-start.5 = (bf16[3,8,4096]{2,1,0:T(8,128)(2,1)S(1)}, bf16[3,8,4096]{2,1,0:T(8,128)(2,1)S(1)}, u32[]{:S(2)}, u32[]{:S(2)}) collective-permute-start(bf16[3,8,4096]{2,1,0:T(8,128)(2,1)S(1)} %get-tuple-element.38), channel_id=1, source_target_pairs={{8,0},{16,8},{24,16},{9,1},{17,9},{25,17},{10,2},{18,10},{26,18},{... | collective-permute-start | bytes 589832 | tf_op jit(solution)/shard_map/ppermute | solution.py:35
  15.6 13.4 collective-permute-start.9
  31.6 16.8 %collective-permute-start.6 = (bf16[24,4096]{1,0:T(8,128)(2,1)S(1)}, bf16[24,4096]{1,0:T(8,128)(2,1)S(1)}, u32[]{:S(2)}, u32[]{:S(2)}) collective-permute-start(bf16[24,4096]{1,0:T(8,128)(2,1)S(1)} %get-tuple-element.36), channel_id=1, source_target_pairs={{0,1},{1,2},{2,3},{3,4},{4,5},{5,6},{6,7},{8,9},{9,10},{10,11},{11... | collective-permute-start | bytes 589832 | tf_op jit(solution)/shard_map/ppermute | solution.py:35
  36.0 12.4 collective-permute-start.7
  37.6 75.3 %collective-permute-start.10 = (f32[34,1,1024]{2,1,0:T(1,128)S(1)}, f32[34,1,1024]{2,1,0:T(1,128)S(1)}, u32[]{:S(2)}, u32[]{:S(2)}) collective-permute-start(f32[34,1,1024]{2,1,0:T(1,128)S(1)} %get-tuple-element.12), channel_id=1, source_target_pairs={{1,0},{2,1},{3,2},{4,3},{5,4},{6,5},{7,6},{9,8},{10,9},{11,10},{12... | collective-permute-start | bytes 417800 | tf_op jit(solution)/shard_map/ppermute | solution.py:27
  38.9 74.0 %collective-permute-start.11 = (f32[34,1,1024]{2,1,0:T(1,128)S(1)}, f32[34,1,1024]{2,1,0:T(1,128)S(1)}, u32[]{:S(2)}, u32[]{:S(2)}) collective-permute-start(f32[34,1,1024]{2,1,0:T(1,128)S(1)} %get-tuple-element.13), channel_id=1, source_target_pairs={{0,1},{1,2},{2,3},{3,4},{4,5},{5,6},{6,7},{8,9},{9,10},{10,11},{11... | collective-permute-start | bytes 417800 | tf_op jit(solution)/shard_map/ppermute | solution.py:26
  140.3 11.0 collective-permute-start.15
  171.1 10.9 collective-permute-start.16
  176.0 367.3 %collective-permute-start.20 = (f32[1,16,512]{2,1,0:T(8,128)}, f32[1,16,512]{2,1,0:T(8,128)}, u32[]{:S(2)}, u32[]{:S(2)}) collective-permute-start(f32[1,16,512]{2,1,0:T(8,128)} %broadcast.350), channel_id=1, source_target_pairs={{8,0},{16,8},{24,16},{9,1},{17,9},{25,17},{10,2},{18,10},{26,18},{... | collective-permute-start | bytes 98312 | tf_op jit(solution)/shard_map/ppermute | solution.py:27
  177.3 366.1 %collective-permute-start.21 = (f32[1,16,512]{2,1,0:T(8,128)}, f32[1,16,512]{2,1,0:T(8,128)}, u32[]{:S(2)}, u32[]{:S(2)}) collective-permute-start(f32[1,16,512]{2,1,0:T(8,128)} %broadcast.350), channel_id=1, source_target_pairs={{0,8},{8,16},{16,24},{1,9},{9,17},{17,25},{2,10},{10,18},{18,26},{... | collective-permute-start | bytes 98312 | tf_op jit(solution)/shard_map/ppermute | solution.py:26
  185.2 367.6 %collective-permute-start.18 = (f32[34,1,1024]{2,1,0:T(1,128)}, f32[34,1,1024]{2,1,0:T(1,128)}, u32[]{:S(2)}, u32[]{:S(2)}) collective-permute-start(f32[34,1,1024]{2,1,0:T(1,128)} %get-tuple-element.8), channel_id=1, source_target_pairs={{1,0},{2,1},{3,2},{4,3},{5,4},{6,5},{7,6},{9,8},{10,9},{11,10},{12... | collective-permute-start | bytes 417800 | tf_op jit(solution)/shard_map/ppermute | solution.py:27
  186.5 366.4 %collective-permute-start.19 = (f32[34,1,1024]{2,1,0:T(1,128)}, f32[34,1,1024]{2,1,0:T(1,128)}, u32[]{:S(2)}, u32[]{:S(2)}) collective-permute-start(f32[34,1,1024]{2,1,0:T(1,128)} %get-tuple-element.9), channel_id=1, source_target_pairs={{0,1},{1,2},{2,3},{3,4},{4,5},{5,6},{6,7},{8,9},{9,10},{10,11},{11... | collective-permute-start | bytes 417800 | tf_op jit(solution)/shard_map/ppermute | solution.py:26
  545.7 379.1 %collective-permute-start.22 = (f32[18,1,512]{2,1,0:T(1,128)}, f32[18,1,512]{2,1,0:T(1,128)}, u32[]{:S(2)}, u32[]{:S(2)}) collective-permute-start(f32[18,1,512]{2,1,0:T(1,128)} %get-tuple-element.32), channel_id=1, source_target_pairs={{1,0},{2,1},{3,2},{4,3},{5,4},{6,5},{7,6},{9,8},{10,9},{11,10},{12... | collective-permute-start | bytes 110600 | tf_op jit(solution)/shard_map/ppermute | solution.py:27
  547.0 377.8 %collective-permute-start.23 = (f32[18,1,512]{2,1,0:T(1,128)}, f32[18,1,512]{2,1,0:T(1,128)}, u32[]{:S(2)}, u32[]{:S(2)}) collective-permute-start(f32[18,1,512]{2,1,0:T(1,128)} %get-tuple-element.33), channel_id=1, source_target_pairs={{0,1},{1,2},{2,3},{3,4},{4,5},{5,6},{6,7},{8,9},{9,10},{10,11},{11... | collective-permute-start | bytes 110600 | tf_op jit(solution)/shard_map/ppermute | solution.py:26
  939.7 11.7 collective-permute-start.28
  941.0 10.4 collective-permute-start.29
  944.4 13.9 %collective-permute-start.32 = (f32[1,8,256]{2,1,0:T(8,128)S(1)}, f32[1,8,256]{2,1,0:T(8,128)S(1)}, u32[]{:S(2)}, u32[]{:S(2)}) collective-permute-start(f32[1,8,256]{2,1,0:T(8,128)S(1)} %broadcast.354), channel_id=1, source_target_pairs={{8,0},{16,8},{24,16},{9,1},{17,9},{25,17},{10,2},{18,10},{26,18},{... | collective-permute-start | bytes 24584 | tf_op jit(solution)/shard_map/ppermute | solution.py:27
  945.7 12.6 collective-permute-start.33
  951.5 13.9 %collective-permute-start.30 = (f32[18,1,512]{2,1,0:T(1,128)S(1)}, f32[18,1,512]{2,1,0:T(1,128)S(1)}, u32[]{:S(2)}, u32[]{:S(2)}) collective-permute-start(f32[18,1,512]{2,1,0:T(1,128)S(1)} %get-tuple-element.28), channel_id=1, source_target_pairs={{1,0},{2,1},{3,2},{4,3},{5,4},{6,5},{7,6},{9,8},{10,9},{11,10},{12... | collective-permute-start | bytes 110600 | tf_op jit(solution)/shard_map/ppermute | solution.py:27
  952.8 12.6 collective-permute-start.31
  958.4 101.7 %collective-permute-start.34 = (f32[10,1,256]{2,1,0:T(1,128)S(1)}, f32[10,1,256]{2,1,0:T(1,128)S(1)}, u32[]{:S(2)}, u32[]{:S(2)}) collective-permute-start(f32[10,1,256]{2,1,0:T(1,128)S(1)} %get-tuple-element.58), channel_id=1, source_target_pairs={{1,0},{2,1},{3,2},{4,3},{5,4},{6,5},{7,6},{9,8},{10,9},{11,10},{12... | collective-permute-start | bytes 30728 | tf_op jit(solution)/shard_map/ppermute | solution.py:27
  959.7 100.4 %collective-permute-start.35 = (f32[10,1,256]{2,1,0:T(1,128)S(1)}, f32[10,1,256]{2,1,0:T(1,128)S(1)}, u32[]{:S(2)}, u32[]{:S(2)}) collective-permute-start(f32[10,1,256]{2,1,0:T(1,128)S(1)} %get-tuple-element.59), channel_id=1, source_target_pairs={{0,1},{1,2},{2,3},{3,4},{4,5},{5,6},{6,7},{8,9},{9,10},{10,11},{11... | collective-permute-start | bytes 30728 | tf_op jit(solution)/shard_map/ppermute | solution.py:26
  1074.0 11.7 collective-permute-start.40
  1078.7 13.8 %collective-permute-start.44 = (f32[1,4,128]{2,1,0:T(4,128)S(1)}, f32[1,4,128]{2,1,0:T(4,128)S(1)}, u32[]{:S(2)}, u32[]{:S(2)}) collective-permute-start(f32[1,4,128]{2,1,0:T(4,128)S(1)} %broadcast.358), channel_id=1, source_target_pairs={{8,0},{16,8},{24,16},{9,1},{17,9},{25,17},{10,2},{18,10},{26,18},{... | collective-permute-start | bytes 6152 | tf_op jit(solution)/shard_map/ppermute | solution.py:27
  1080.0 12.5 collective-permute-start.45
  1085.8 14.0 %collective-permute-start.42 = (f32[10,1,256]{2,1,0:T(1,128)S(1)}, f32[10,1,256]{2,1,0:T(1,128)S(1)}, u32[]{:S(2)}, u32[]{:S(2)}) collective-permute-start(f32[10,1,256]{2,1,0:T(1,128)S(1)} %get-tuple-element.54), channel_id=1, source_target_pairs={{1,0},{2,1},{3,2},{4,3},{5,4},{6,5},{7,6},{9,8},{10,9},{11,10},{12... | collective-permute-start | bytes 30728 | tf_op jit(solution)/shard_map/ppermute | solution.py:27
  1087.1 12.8 collective-permute-start.43
  1092.6 23.5 %collective-permute-start.46 = (f32[6,1,128]{2,1,0:T(1,128)S(1)}, f32[6,1,128]{2,1,0:T(1,128)S(1)}, u32[]{:S(2)}, u32[]{:S(2)}) collective-permute-start(f32[6,1,128]{2,1,0:T(1,128)S(1)} %get-tuple-element.76), channel_id=1, source_target_pairs={{1,0},{2,1},{3,2},{4,3},{5,4},{6,5},{7,6},{9,8},{10,9},{11,10},{12... | collective-permute-start | bytes 9224 | tf_op jit(solution)/shard_map/ppermute | solution.py:27
  1093.9 22.2 %collective-permute-start.47 = (f32[6,1,128]{2,1,0:T(1,128)S(1)}, f32[6,1,128]{2,1,0:T(1,128)S(1)}, u32[]{:S(2)}, u32[]{:S(2)}) collective-permute-start(f32[6,1,128]{2,1,0:T(1,128)S(1)} %get-tuple-element.77), channel_id=1, source_target_pairs={{0,1},{1,2},{2,3},{3,4},{4,5},{5,6},{6,7},{8,9},{9,10},{10,11},{11... | collective-permute-start | bytes 9224 | tf_op jit(solution)/shard_map/ppermute | solution.py:26
  (67 other events, 816.1 us)
where the time goes:
time: 1370 us; the launch traced here: 1350 us
  local copies, waits for them, and re-layouts  738 us (54%)
  other arithmetic  304 us (22%)
  starting transfers between devices  258 us (19%)
  waiting for transfers between devices  41.2 us (3%)
    reshape x4, local copies, waits for them, and re-layouts, shrink(): values.reshape(zsize // 2, 2, xsize // 2, 2, ysize // 2, 2)  581 us
    reduce_sum x6, other arithmetic, shrink(): values.reshape(zsize // 2, 2, xsize // 2, 2, ysize // 2, 2)  191 us
    ppermute x38, starting transfers between devices, extended(): before = lax.ppermute(last, axis, up)  188 us
    add x13, other arithmetic, smooth_once(): values + OMEGA * (source - operate(values, diagonal, spread)) / diagonal  76 us
    ppermute x38, starting transfers between devices, extended(): after = lax.ppermute(initial, axis, down)  49.6 us
    div x2, local copies, waits for them, and re-layouts, shrink(): values.reshape(zsize // 2, 2, xsize // 2, 2, ysize // 2, 2)  40.4 us
    ppermute x38, waiting for transfers between devices, extended(): before = lax.ppermute(last, axis, up)  31.5 us
    reshape x1, local copies, waits for them, and re-layouts, shards(): secretion = gathered.reshape(per_z, per_x, per_y, EDGE, EDGE, EDGE).trans...  28.3 us
  transfers between devices with their start and end apart: 84, of which 29 were waited for; matrix products, arithmetic and copies ran while one was open for 68% of the time, Pallas kernels for 0%

commit v1 on v0

v1 whole, which is shorter than its diff:
```python
import jax
import jax.numpy as jnp
from jax import lax
from jax.experimental import pallas as pl
from jax.experimental.pallas import tpu as pltpu
from jax.sharding import PartitionSpec as P

EDGE = 16
CAP = 8
BRICK = 4096
SLOTS = 72
KAPPA = 32.0
OMEGA = 0.8
KEEP = 1.0 - OMEGA

C = 32
NT = 8
F32 = jnp.float32
BF16 = jnp.bfloat16


def spread(level):
    return KAPPA / 4.0**level


def shifted(values, distance, axis):
    return pltpu.roll(values, distance % values.shape[axis], axis)


def iota(shape, dim):
    return lax.broadcasted_iota(jnp.int32, shape, dim)


def lanes(t):
    return slice(t * 128, (t + 1) * 128)


def along_y(tiles):
    lane = iota(tiles[0].shape, 1)
    ahead = [shifted(a, 1, 1) for a in tiles]
    behind = [shifted(a, -1, 1) for a in tiles]
    sums = []
    for t in range(len(tiles)):
        low = ahead[t - 1] if t else 0.0
        high = behind[t + 1] if t + 1 < len(tiles) else 0.0
        sums.append(jnp.where(lane == 0, low, ahead[t]) + jnp.where(lane == 127, high, behind[t]))
    return sums


def plane(ref, p):
    count = ref.shape[2] // 128
    here = [ref[p, :, lanes(t)] for t in range(count)]
    sums = along_y(here)
    for t in range(count):
        near = ref[p - 1, :, lanes(t)] + ref[p + 1, :, lanes(t)]
        near = near + (shifted(here[t], 1, 0) + shifted(here[t], -1, 0))
        sums[t] = sums[t] + near
    return here, sums


def loop(start, stop, body):
    def step(i, carry):
        body(i)
        return carry

    lax.fori_loop(start, stop, step, 0)


def split_dot(a, b):
    high = a.astype(BF16)
    low = (a - high.astype(F32)).astype(BF16)
    return jnp.dot(high, b, preferred_element_type=F32) + jnp.dot(low, b, preferred_element_type=F32)


def pooling():
    return jnp.where(iota((256, 128), 0) // 2 == iota((256, 128), 1), 0.125, 0.0).astype(BF16)


def doubling():
    return jnp.where(iota((128, 256), 1) // 2 == iota((128, 256), 0), 1.0, 0.0).astype(BF16)


def halve_rows(values, rs, t):
    rows = values.shape[0]
    rs[t, 0:rows, :] = values
    return rs[t, pl.ds(0, rows // 2, stride=2), :] + rs[t, pl.ds(1, rows // 2, stride=2), :]


def halve_lanes(xp, planes, rows):
    matrix = pooling()
    tiles = []
    for t in range(0, xp.shape[0], 2):
        pair = jnp.concatenate([xp[t].reshape(planes * rows, 128), xp[t + 1].reshape(planes * rows, 128)], axis=1)
        tiles.append(split_dot(pair, matrix).reshape(planes, rows, 128))
    return tiles


def inside(shape, dim, first, wrap, index, size, count):
    place = iota(shape, dim) + first
    if wrap is not None:
        place = jnp.where(place < wrap, place, place - shape[dim])
    place = place + index * size
    return (place >= 0) & (place < count * size)


def brick_kernel(bricks_x, ids, counts, bricks, out, xs):
    xs[...] = bricks[...].astype(F32)
    row = iota((1, 8, 128), 1)
    group = iota((1, 8, 128), 2) // 16
    group16 = iota((16, 128), 1) // 16
    per_y = 64

    def block(j):
        start = pl.multiple_of(j * 8, 8)
        x = jnp.stack([xs[pl.ds(start, 8), lanes(k)] for k in range(32)])
        for s in (4, 2, 1):
            up = shifted(shifted(x, -s, 1), 16 * s, 2)
            down = shifted(shifted(x, s, 1), -16 * s, 2)
            row_bit = (row // s) % 2
            group_bit = (group // s) % 2
            x = jnp.where(row_bit == group_bit, x, jnp.where(row_bit == 0, up, down))
        x = jnp.where(group < counts[0, j], x, 0.0)
        out[j, 0:256, :] = x.reshape(256, 128).astype(BF16)
        names = jnp.zeros((16, 128), jnp.int32)
        for e in range(CAP):
            number = ids[j * 8 + e]
            by = lax.rem(number, per_y)
            rest = lax.div(number, per_y)
            bx = lax.rem(rest, 2)
            bz = lax.rem(lax.div(rest, bricks_x), 2)
            names = jnp.where(group16 == e, (bz * 2 + bx) * per_y + by, names)
        out[j, 256:272, :] = names.astype(F32).astype(BF16)

    loop(0, 9, block)


def rates_kernel(uptake, r1, r2, rs, xp, rs1, xp1):
    def pair(m):
        for t in range(NT):
            both = uptake[2 * m, :, lanes(t)] + uptake[2 * m + 1, :, lanes(t)]
            xp[t, m] = halve_rows(both, rs, t)

    loop(0, 16, pair)
    for t, tile in enumerate(halve_lanes(xp, 16, 16)):
        r1[:, :, lanes(t)] = tile

    def pair1(m):
        for t in range(4):
            both = r1[2 * m, :, lanes(t)] + r1[2 * m + 1, :, lanes(t)]
            xp1[t, m] = halve_rows(both, rs1, t)

    loop(0, 8, pair1)
    for t, tile in enumerate(halve_lanes(xp1, 8, 8)):
        r2[:, lanes(t)] = tile.reshape(64, 128)


def pre_kernel(
    nz, nx, info, density, uptake, uzl, uzh, uxl, uxr, own, zl, zh, xl, xr, r1,
    supply, c1, mzl, mzh, vzl, vzh, pxl, pxh, v_out, g_out,
    va, vb, dd, gg, hot, rs, xp, sems,
):
    iz, ix = info[0], info[1]
    k = spread(0)
    base = 1.0 + 6.0 * k
    O = 5
    Q = 2

    for p in (0, 1, 2, 3, 4, 37, 38, 39, 40, 41):
        va[p] = jnp.zeros((40, 1024), F32)
    for p in (2, 3, 38, 39):
        vb[p] = jnp.zeros((40, 1024), F32)

    sub8 = iota((8, 1024), 0)

    def set_plane(q, rates, valid_z):
        gz = jnp.where(valid_z, OMEGA, 0.0)
        d = rates + base
        dd[q, 0:32, :] = d
        gg[q, 0:32, :] = gz / d
        high = jnp.concatenate([uxr[q], jnp.zeros((6, 1024), F32)], axis=0)
        low = jnp.concatenate([jnp.zeros((6, 1024), F32), uxl[q]], axis=0)
        d = high + low + base
        dd[q, 32:40, :] = d
        omega = jnp.where(sub8 < 2, jnp.where(ix < nx - 1, gz, 0.0), jnp.where(sub8 >= 6, jnp.where(ix > 0, gz, 0.0), 0.0))
        gg[q, 32:40, :] = omega / d

    def own_plane(z):
        va[z + O, 0:32, :] = density[z]
        va[z + O, 32:40, :] = jnp.zeros((8, 1024), F32)
        set_plane(z + Q, uptake[z], True)

    loop(0, C, own_plane)
    for i in range(2):
        set_plane(i, uzl[i].astype(F32), iz > 0)
        set_plane(34 + i, uzh[i].astype(F32), iz < nz - 1)

    blocks = [own.at[4], zl.at[1], zh.at[1]] + [xl.at[i] for i in range(3)] + [xr.at[i] for i in range(3)]
    lane = iota((1, 128), 1)
    at_y = iota((1024, 128), 0)
    tiles = []
    for i, ref in enumerate(blocks):
        name = ref[256:272, :].astype(F32).astype(jnp.int32)[0:1]
        tiles.append(lax.shift_right_logical(name, 6))
        y = (name & 63) * 16 + (lane & 15)
        hot[:, lanes(i)] = jnp.where(at_y == y, 1.0, 0.0).astype(BF16)
    for tile in range(4):
        bz, bx = tile // 2, tile % 2
        left = jnp.concatenate(
            [jnp.where(tiles[i] == tile, ref[0:256, :].astype(F32), 0.0).astype(BF16) for i, ref in enumerate(blocks)],
            axis=1,
        )
        for n in range(4):
            cols = slice(n * 256, (n + 1) * 256)
            part = lax.dot_general(left, hot[cols, :], (((1,), (1,)), ((), ())), preferred_element_type=F32)
            zs, xs = slice(16 * bz, 16 * bz + 16), slice(16 * bx, 16 * bx + 16)
            supply[zs, xs, cols] = density[zs, xs, cols] + part.reshape(16, 16, 256)

    def sweep(src, dst, z, sourced):
        here, sums = plane(src, z + O)
        for t in range(NT):
            inner = k * sums[t]
            g = gg[z + Q, :, lanes(t)]
            if sourced:
                body = inner[0:32] + supply[z, :, lanes(t)]
                dst[z + O, 0:32, lanes(t)] = KEEP * here[t][0:32] + g[0:32] * body
                dst[z + O, 32:40, lanes(t)] = KEEP * here[t][32:40] + g[32:40] * inner[32:40]
            else:
                dst[z + O, :, lanes(t)] = KEEP * here[t] + g * inner

    def halo_planes(src, dst, width):
        def step(i):
            sweep(src, dst, jnp.where(i < width, i - width, i - width + C), False)

        loop(0, 2 * width, step)

    loop(0, C, lambda z: sweep(va, vb, z, True))
    halo_planes(va, vb, 1)
    loop(0, C, lambda z: sweep(vb, va, z, True))
    halo_planes(vb, va, 2)

    v_copy = pltpu.make_async_copy(va.at[3:39], v_out, sems.at[0])
    g_copy = pltpu.make_async_copy(gg, g_out, sems.at[1])
    v_copy.start()
    g_copy.start()

    def residual(z, sourced, edge):
        here, sums = plane(va, z + O)
        out = []
        for t in range(NT):
            r = k * sums[t]
            if not edge:
                r = r - dd[z + Q, :, lanes(t)] * here[t]
            if sourced:
                r = jnp.concatenate([r[0:32] + supply[z, :, lanes(t)], r[32:40]], axis=0)
            out.append(r)
        return out

    def coarse(m, sourced):
        first = residual(2 * m - 4, sourced, False)
        second = residual(2 * m - 3, sourced, False)
        for t in range(NT):
            xp[t, m, 0:20, :] = halve_rows(first[t] + second[t], rs, t)

    loop(2, 18, lambda m: coarse(m, True))
    loop(0, 2, lambda i: coarse(1 + 17 * i, False))

    def outer(i):
        r = residual(jnp.where(i == 0, -3, 34), False, True)
        for t in range(NT):
            xp[t, 19 * i, 0:20, :] = halve_rows(r[t], rs, t)

    loop(0, 2, outer)

    sub = iota((20, 8, 128), 1)
    for t, tile in enumerate(halve_lanes(xp, 20, 24)):
        last = tile[:, 16:24]
        last = jnp.where(sub < 2, last, jnp.where(sub >= 6, shifted(last, 4, 1), 0.0))
        c1[:, 0:16, lanes(t)] = tile[:, 0:16]
        c1[:, 16:24, lanes(t)] = last

    blank = jnp.zeros((4, 8, 512), F32)
    low = jnp.concatenate([c1[0:6], jnp.concatenate([r1[0:4], blank], axis=1)], axis=0)
    mzl[...] = low.reshape(240, 512).astype(BF16)
    high = jnp.concatenate([c1[14:20], jnp.concatenate([r1[12:16], blank], axis=1)], axis=0)
    mzh[...] = high.reshape(240, 512).astype(BF16)

    empty = jnp.zeros((1, 8, 1024), F32)
    low = jnp.concatenate([va[3:7], jnp.concatenate([supply[0:1], empty], axis=1)], axis=0)
    vzl[...] = low.reshape(200, 1024).astype(BF16)
    high = jnp.concatenate([va[35:39], jnp.concatenate([supply[31:32], empty], axis=1)], axis=0)
    vzh[...] = high.reshape(200, 1024).astype(BF16)

    def sides(i):
        lows, highs = [], []
        for j in range(2):
            p = 2 * i + j
            z = p - 2
            held = jnp.where((z >= 0) & (z < C), 1.0, 0.0)
            zc = jnp.clip(z, 0, C - 1)
            f_low = shifted(supply[zc, 0:8, :], 4, 0) * held
            f_high = shifted(supply[zc, 24:32, :], 5, 0) * held
            first, last, halo = va[p + 3, 0:8, :], va[p + 3, 24:32, :], va[p + 3, 32:40, :]
            lows.append(pack_low(sub8, first, halo, f_low))
            highs.append(pack_high(sub8, last, halo, f_high))
        rows = pl.ds(pl.multiple_of(16 * i, 16), 16)
        pxl[rows, :] = jnp.concatenate(lows, axis=0).astype(BF16)
        pxh[rows, :] = jnp.concatenate(highs, axis=0).astype(BF16)

    loop(0, 18, sides)
    v_copy.wait()
    g_copy.wait()


def pack_low(sub, first, halo, f):
    return jnp.where(sub < 2, first, jnp.where(sub >= 6, halo, jnp.where(sub == 4, f, 0.0)))


def pack_high(sub, last, halo, f):
    return jnp.where(sub >= 6, last, jnp.where(sub < 2, halo, jnp.where(sub == 4, f, 0.0)))


def sides_kernel(pxl, pxh, vzl, vzh, out_l, out_h):
    sub = iota((8, 1024), 0)
    for ref, out, low_side in ((pxl, out_l, True), (pxh, out_h, False)):
        out[...] = ref[...]
        for message, start, f_plane in ((vzl, 0, 1), (vzh, 32, 2)):
            planes = message[...].astype(F32).reshape(5, 40, 1024)
            for pair in range(2):
                added = []
                for i in (2 * pair, 2 * pair + 1):
                    v, f = planes[i], planes[4]
                    f_low = shifted(f[0:8], 4, 0) if i == f_plane else 0.0
                    f_high = shifted(f[24:32], 5, 0) if i == f_plane else 0.0
                    if low_side:
                        added.append(pack_low(sub, v[0:8], v[32:40], f_low))
                    else:
                        added.append(pack_high(sub, v[24:32], v[32:40], f_high))
                rows = slice((start + 2 * pair) * 8, (start + 2 * pair) * 8 + 16)
                total = ref[rows, :].astype(F32) + jnp.concatenate(added, axis=0)
                out[rows, :] = total.astype(BF16)


def merge_kernel(c1, r1, mzl, mzh, f1, q1, mxl, mxh):
    zeros = jnp.zeros((24, 512), F32)
    for p in (0, 1, 22, 23):
        f1[p] = zeros
    f1[2:22] = c1[...]
    low = mzl[...].astype(F32).reshape(10, 24, 512)
    high = mzh[...].astype(F32).reshape(10, 24, 512)
    f1[0:6] = f1[0:6] + low[0:6]
    f1[18:24] = f1[18:24] + high[0:6]
    q1[0:4] = low[6:10]
    q1[20:24] = high[6:10]
    q1[4:20, 0:16, :] = r1[...]
    q1[4:20, 16:24, :] = jnp.zeros((16, 8, 512), F32)
    sub = iota((24, 8, 512), 1)
    first, last, halo = f1[:, 0:8], f1[:, 8:16], f1[:, 16:24]
    to_high = jnp.where(sub >= 4, last, jnp.where(sub < 2, halo, 0.0))
    to_low = jnp.where(sub >= 6, halo, jnp.where(sub < 4, first, 0.0))
    mxh[0:192, :] = to_high.reshape(192, 512).astype(BF16)
    mxh[192:384, :] = q1[:, 8:16].reshape(192, 512).astype(BF16)
    mxl[0:192, :] = to_low.reshape(192, 512).astype(BF16)
    mxl[192:384, :] = q1[:, 0:8].reshape(192, 512).astype(BF16)


def middle_kernel(nz, nx, info, f0, q0, mxl, mxh, f1, g1, v1, g2, va, rs, xp):
    iz, ix = info[0], info[1]
    k = spread(1)
    base = 1.0 + 6.0 * k
    low = mxl[...].astype(F32).reshape(48, 8, 512)
    high = mxh[...].astype(F32).reshape(48, 8, 512)
    sub = iota((24, 8, 512), 1)
    f1[:, 0:8] = f0[:, 0:8] + jnp.where(sub < 2, low[0:24], 0.0)
    f1[:, 8:16] = f0[:, 8:16] + jnp.where(sub >= 6, high[0:24], 0.0)
    f1[:, 16:24] = f0[:, 16:24] + jnp.where(sub >= 4, low[0:24], high[0:24])
    q0[:, 16:24] = jnp.where(sub >= 4, low[24:48], high[24:48])
    shape = (24, 24, 128)
    valid = inside(shape, 0, -4, None, iz, 16, nz) & inside(shape, 1, 0, 20, ix, 16, nx)
    for t in range(4):
        g = jnp.where(valid, OMEGA, 0.0) / (q0[:, :, lanes(t)] + base)
        g1[:, :, lanes(t)] = g
        va[:, :, lanes(t)] = g * f1[:, :, lanes(t)]
    v1[0] = va[0]
    v1[23] = va[23]

    def sweep(p):
        here, sums = plane(va, p)
        for t in range(4):
            v1[p, :, lanes(t)] = KEEP * here[t] + g1[p, :, lanes(t)] * (f1[p, :, lanes(t)] + k * sums[t])

    loop(1, 23, sweep)

    def coarse(m):
        total = None
        for j in range(2):
            p = 2 * m + 4 + j
            here, sums = plane(v1, p)
            r = [
                f1[p, :, lanes(t)] + k * sums[t] - (q0[p, :, lanes(t)] + base) * here[t]
                for t in range(4)
            ]
            total = r if total is None else [a + b for a, b in zip(total, r)]
        for t in range(4):
            xp[t, m] = halve_rows(total[t][0:16], rs, t)

    loop(0, 8, coarse)
    for t, tile in enumerate(halve_lanes(xp, 8, 8)):
        g2[:, lanes(t)] = tile.reshape(64, 128)


def back_kernel(
    nz, nx, info, f1, g1, v1, vzl, vzh, vxl, vxh, g2, r2, v_in, g_in, s_in,
    out,
    f2, q2, h2, a2, b2, rs, xp, xpr, wa, w1, zsl, zsh, vb, ws,
    g2s, r2s, v2, gg, supply, sems, sems2,
):
    iz, ix = info[0], info[1]
    matrix = doubling()

    x_first = jnp.clip(ix - 2, 0, nx - 5)
    near = []
    for dz in range(5):
        at = pl.ds(jnp.clip(iz + dz - 2, 0, nz - 1) * nx + x_first, 5)
        near.append(pltpu.make_async_copy(g2.at[at], g2s.at[dz], sems2.at[0, dz]))
        near.append(pltpu.make_async_copy(r2.at[at], r2s.at[dz], sems2.at[1, dz]))
    level0 = [
        pltpu.make_async_copy(src, dst, sems.at[i])
        for i, (src, dst) in enumerate(((v_in, v2), (g_in, gg), (s_in, supply)))
    ]
    for copy in near + level0:
        copy.start()
    for copy in near:
        copy.wait()

    sub4 = iota((8, 8, 256), 1)
    for dz in range(-2, 3):
        lo = 4 if dz == -2 else 0
        hi = 4 if dz == 2 else 8
        planes = slice(12 + 8 * dz + lo, 12 + 8 * dz + hi)
        for src, ref in ((g2s, f2), (r2s, q2)):
            parts = {}
            for dx in range(-2, 3):
                at = jnp.clip(ix + dx, 0, nx - 1) - x_first
                parts[dx] = src[dz + 2, at].reshape(8, 8, 256)
            far = jnp.where(sub4 < 4, parts[2], parts[-2])
            for n, tile in enumerate((parts[0], parts[1], far, parts[-1])):
                ref[planes, 8 * n : 8 * n + 8, :] = tile[lo:hi]

    k = spread(2)
    base = 1.0 + 6.0 * k
    shape = (32, 32, 128)
    valid = inside(shape, 0, -12, None, iz, 8, nz) & inside(shape, 1, 0, 20, ix, 8, nx)
    for t in range(2):
        g = jnp.where(valid, OMEGA, 0.0) / (q2[:, :, lanes(t)] + base)
        h2[:, :, lanes(t)] = g
        a2[:, :, lanes(t)] = g * f2[:, :, lanes(t)]
    b2[0] = a2[0]
    b2[31] = a2[31]

    def sweep2(src, dst):
        def body(p):
            here, sums = plane(src, p)
            for t in range(2):
                dst[p, :, lanes(t)] = KEEP * here[t] + h2[p, :, lanes(t)] * (f2[p, :, lanes(t)] + k * sums[t])

        return body

    loop(1, 31, sweep2(a2, b2))

    def coarse(m):
        total, rates = [0.0, 0.0], [0.0, 0.0]
        for j in range(2):
            p = 2 * m + j
            here, sums = plane(b2, p)
            for t in range(2):
                r = f2[p, :, lanes(t)] + k * sums[t] - (q2[p, :, lanes(t)] + base) * here[t]
                total[t] = total[t] + r
                rates[t] = rates[t] + q2[p, :, lanes(t)]
        for t in range(2):
            xp[t, m] = halve_rows(total[t], rs, t)
            xpr[t, m] = halve_rows(rates[t], rs, t + 2)

    for t in range(2):
        for m in (0, 15):
            xp[t, m] = jnp.zeros((16, 128), F32)
            xpr[t, m] = jnp.zeros((16, 128), F32)
    loop(1, 15, coarse)

    shape = (16, 16, 128)
    valid = inside(shape, 0, -6, None, iz, 4, nz) & inside(shape, 1, 0, 10, ix, 4, nx)
    k3 = spread(3)
    (source,) = halve_lanes(xp, 16, 16)
    (rates,) = halve_lanes(xpr, 16, 16)
    g = jnp.where(valid, OMEGA, 0.0) / (rates + (1.0 + 6.0 * k3))
    v = g * source
    lane = iota(shape, 2)
    for repeat in range(3):
        edge = jnp.zeros((1, 16, 128), F32)
        sums = jnp.concatenate([v[1:], edge], axis=0) + jnp.concatenate([edge, v[:-1]], axis=0)
        sums = sums + shifted(v, 1, 1) + shifted(v, -1, 1)
        sums = sums + jnp.where(lane == 0, 0.0, shifted(v, 1, 2)) + jnp.where(lane == 127, 0.0, shifted(v, -1, 2))
        v = KEEP * v + g * (source + k3 * sums)

    wide = split_dot(v[4:12].reshape(128, 128), matrix).reshape(8, 16, 256)
    for m in range(8):
        for t in range(2):
            part = wide[m, :, lanes(t)]
            rs[t, pl.ds(0, 16, stride=2), :] = part
            rs[t, pl.ds(1, 16, stride=2), :] = part
            for j in range(2):
                p = 8 + 2 * m + j
                b2[p, :, lanes(t)] = b2[p, :, lanes(t)] + rs[t, 0:32, :]
    loop(9, 23, sweep2(b2, a2))
    loop(10, 22, sweep2(a2, b2))

    w = b2[10:22]
    near, far = w[:, 8:16], w[:, 24:32]
    near = jnp.where(iota((12, 8, 256), 1) < 2, near, shifted(far, 4, 1))
    w = jnp.concatenate([w[:, 0:8], near], axis=1).reshape(192, 256)
    wide = [split_dot(w[:, lanes(t)], matrix) for t in range(2)]
    wide = jnp.concatenate(wide, axis=1).reshape(12, 16, 512)
    for m in range(12):
        for t in range(4):
            part = wide[m, :, lanes(t)]
            rs[t, pl.ds(0, 16, stride=2), :] = part
            rs[t, pl.ds(1, 16, stride=2), :] = part
            for j in range(2):
                p = 2 * m + j
                wa[p, :, lanes(t)] = v1[p, :, lanes(t)] + rs[t, 0:24, :]
    k1 = spread(1)

    def sweep1(src, dst):
        def body(p):
            here, sums = plane(src, p)
            for t in range(4):
                dst[p, :, lanes(t)] = KEEP * here[t] + g1[p, :, lanes(t)] * (f1[p, :, lanes(t)] + k1 * sums[t])

        return body

    loop(2, 22, sweep1(wa, w1))
    loop(3, 21, sweep1(w1, wa))

    sub = iota((18, 8, 128), 1)
    for t in range(4):
        halo = wa[3:21, 16:24, lanes(t)]
        halo = jnp.where(sub < 2, halo, shifted(halo, 4, 1))
        w = jnp.concatenate([wa[3:21, 0:16, lanes(t)], halo], axis=1)
        ws[:, :, t * 256 : t * 256 + 256] = split_dot(w.reshape(432, 128), matrix).reshape(18, 24, 256)

    for copy in level0:
        copy.wait()
    zsl[...] = vzl[...].astype(F32)
    zsh[...] = vzh[...].astype(F32)
    for i in range(4):
        v2[i] = v2[i] + zsl[40 * i : 40 * i + 40, :]
        v2[32 + i] = v2[32 + i] + zsh[40 * i : 40 * i + 40, :]

    s8 = iota((8, 128), 0)

    def correct(m):
        rows = pl.ds(pl.multiple_of(16 * m, 16), 16)
        for t in range(NT):
            part = ws[m, :, lanes(t)]
            rs[t, pl.ds(0, 24, stride=2), :] = part
            rs[t, pl.ds(1, 24, stride=2), :] = part
            low = vxl[rows, lanes(t)].astype(F32)
            high = vxh[rows, lanes(t)].astype(F32)
            for j in range(2):
                p = 2 * m + j
                lo, hi = low[8 * j : 8 * j + 8], high[8 * j : 8 * j + 8]
                v2[p, 0:8, lanes(t)] = v2[p, 0:8, lanes(t)] + rs[t, 0:8, :] + jnp.where(s8 < 2, lo, 0.0)
                v2[p, 8:24, lanes(t)] = v2[p, 8:24, lanes(t)] + rs[t, 8:24, :]
                v2[p, 24:32, lanes(t)] = v2[p, 24:32, lanes(t)] + rs[t, 24:32, :] + jnp.where(s8 >= 6, hi, 0.0)
                extra = jnp.where(s8 >= 6, lo, jnp.where(s8 < 2, hi, 0.0))
                v2[p, 32:40, lanes(t)] = v2[p, 32:40, lanes(t)] + rs[t, 32:40, :] + extra

    loop(0, 18, correct)
    k0 = spread(0)

    def first(i):
        rows = pl.ds(pl.multiple_of(16 * i + 16, 16), 16)
        for j in range(2):
            z = 2 * i + j
            here, sums = plane(v2, z + 2)
            for t in range(NT):
                lo = vxl[rows, lanes(t)].astype(F32)[8 * j : 8 * j + 8]
                hi = vxh[rows, lanes(t)].astype(F32)[8 * j : 8 * j + 8]
                f = jnp.where(s8 == 7, shifted(lo, 3, 0), jnp.where(s8 == 0, shifted(hi, 4, 0), 0.0))
                g = gg[z + 2, :, lanes(t)]
                inner = k0 * sums[t]
                vb[z + 1, 0:32, lanes(t)] = KEEP * here[t][0:32] + g[0:32] * (supply[z, :, lanes(t)] + inner[0:32])
                vb[z + 1, 32:40, lanes(t)] = KEEP * here[t][32:40] + g[32:40] * (f + inner[32:40])

    loop(0, 16, first)
    for p, ref in ((1, zsl), (34, zsh)):
        here, sums = plane(v2, p)
        for t in range(NT):
            g = gg[p, :, lanes(t)]
            vb[p - 1, :, lanes(t)] = KEEP * here[t] + g * (ref[160:200, lanes(t)] + k0 * sums[t])

    def second(z):
        here, sums = plane(vb, z + 1)
        for t in range(NT):
            g = gg[z + 2, 0:32, lanes(t)]
            out[z, :, lanes(t)] = KEEP * here[t][0:32] + g * (supply[z, :, lanes(t)] + k0 * sums[t][0:32])

    loop(0, C, second)


VMEM = pl.BlockSpec(memory_space=pltpu.VMEM)
SMEM = pl.BlockSpec(memory_space=pltpu.SMEM)
ANY = pl.BlockSpec(memory_space=pl.ANY)


def call(kernel, outs, scratch, smem, args, out_specs=None, in_hbm=0):
    moved = sum(a.size * a.dtype.itemsize for a in list(args) + list(outs))
    return pl.pallas_call(
        kernel,
        out_shape=tuple(outs),
        in_specs=[SMEM] * smem + [VMEM] * (len(args) - smem - in_hbm) + [ANY] * in_hbm,
        out_specs=tuple(out_specs or [VMEM] * len(outs)),
        scratch_shapes=scratch,
        compiler_params=pltpu.CompilerParams(vmem_limit_bytes=58 * 2**20),
        cost_estimate=pl.CostEstimate(flops=20 * moved, bytes_accessed=moved, transcendentals=0),
    )(*args)


def shaped(shape, dtype=F32):
    return jax.ShapeDtypeStruct(shape, dtype)


def both_ways(to_low, to_high, axis):
    count = lax.axis_size(axis)
    up = [(i, i + 1) for i in range(count - 1)]
    down = [(j, i) for i, j in up]
    return lax.ppermute(to_high, axis, up), lax.ppermute(to_low, axis, down)


def shards(density, uptake, brick_values, brick_ids, slot_counts):
    nz, nx = lax.axis_size("gz"), lax.axis_size("xy")
    info = jnp.stack([lax.axis_index("gz"), lax.axis_index("xy")]).astype(jnp.int32)
    scratch = pltpu.VMEM

    (blocks,) = call(
        lambda *refs: brick_kernel(2 * nx, *refs),
        [shaped((9, 272, 128), BF16)],
        [scratch((SLOTS, BRICK), F32)],
        2,
        (brick_ids, slot_counts, brick_values),
    )
    uzl, uzh = both_ways(uptake[0:2].astype(BF16), uptake[30:32].astype(BF16), "gz")
    zl, zh = both_ways(blocks[0:3], blocks[6:9], "gz")
    r1, r2 = call(
        rates_kernel,
        [shaped((16, 16, 512)), shaped((64, 256))],
        [scratch((8, 32, 128), F32), scratch((8, 16, 16, 128), F32), scratch((4, 16, 128), F32), scratch((4, 8, 8, 128), F32)],
        0,
        (uptake,),
    )
    r2_all = lax.all_gather(r2, ("gz", "xy"))
    column = lambda s: jnp.concatenate([uzl[:, s].astype(F32), uptake[:, s], uzh[:, s].astype(F32)], axis=0)
    uxl, uxr = both_ways(column(slice(0, 2)), column(slice(30, 32)), "xy")
    hop = lambda d: jnp.stack([blocks[3 + d], zl[d], zh[d]])
    xl, xr = both_ways(hop(0), hop(2), "xy")

    supply, c1, mzl, mzh, vzl, vzh, pxl, pxh, v2, gg = call(
        lambda *refs: pre_kernel(nz, nx, *refs),
        [
            shaped((C, C, 1024)),
            shaped((20, 24, 512)),
            shaped((240, 512), BF16),
            shaped((240, 512), BF16),
            shaped((200, 1024), BF16),
            shaped((200, 1024), BF16),
            shaped((288, 1024), BF16),
            shaped((288, 1024), BF16),
            shaped((36, 40, 1024)),
            shaped((36, 40, 1024)),
        ],
        [
            scratch((42, 40, 1024), F32),
            scratch((42, 40, 1024), F32),
            scratch((36, 40, 1024), F32),
            scratch((36, 40, 1024), F32),
            scratch((1024, 1152), BF16),
            scratch((8, 40, 128), F32),
            scratch((8, 20, 24, 128), F32),
            pltpu.SemaphoreType.DMA((2,)),
        ],
        1,
        (info, density, uptake, uzl, uzh, uxl, uxr, blocks, zl, zh, xl, xr, r1),
        [VMEM] * 8 + [ANY] * 2,
    )
    mzl, mzh = both_ways(mzl, mzh, "gz")
    vzl, vzh = both_ways(vzl, vzh, "gz")
    f1, q1, mxl, mxh = call(
        merge_kernel,
        [shaped((24, 24, 512)), shaped((24, 24, 512)), shaped((384, 512), BF16), shaped((384, 512), BF16)],
        [],
        0,
        (c1, r1, mzl, mzh),
    )
    mxl, mxh = both_ways(mxl, mxh, "xy")
    pxl, pxh = call(
        sides_kernel,
        [shaped((288, 1024), BF16), shaped((288, 1024), BF16)],
        [],
        0,
        (pxl, pxh, vzl, vzh),
    )
    f1, g1, v1, g2 = call(
        lambda *refs: middle_kernel(nz, nx, *refs),
        [shaped((24, 24, 512)), shaped((24, 24, 512)), shaped((24, 24, 512)), shaped((64, 256))],
        [scratch((24, 24, 512), F32), scratch((4, 16, 128), F32), scratch((4, 8, 8, 128), F32)],
        1,
        (info, f1, q1, mxl, mxh),
    )
    g2_all = lax.all_gather(g2, ("gz", "xy"))
    vxl, vxh = both_ways(pxl, pxh, "xy")
    window2 = scratch((32, 32, 256), F32)
    window1 = scratch((24, 24, 512), F32)
    (concentration,) = call(
        lambda *refs: back_kernel(nz, nx, *refs),
        [shaped((C, C, 1024))],
        [
            window2, window2, window2, window2, window2,
            scratch((8, 48, 128), F32),
            scratch((2, 16, 16, 128), F32),
            scratch((2, 16, 16, 128), F32),
            window1, window1,
            scratch((200, 1024), F32),
            scratch((200, 1024), F32),
            scratch((34, 40, 1024), F32),
            scratch((18, 24, 1024), F32),
            scratch((5, 5, 64, 256), F32),
            scratch((5, 5, 64, 256), F32),
            scratch((36, 40, 1024), F32),
            scratch((36, 40, 1024), F32),
            scratch((C, C, 1024), F32),
            pltpu.SemaphoreType.DMA((3,)),
            pltpu.SemaphoreType.DMA((2, 5)),
        ],
        1,
        (info, f1, g1, v1, vzl, vzh, vxl, vxh, g2_all, r2_all, v2, gg, supply),
        in_hbm=5,
    )
    return supply, concentration


def solution(mesh):
    return jax.shard_map(
        shards,
        mesh=mesh,
        in_specs=(
            P("gz", "xy", None),
            P("gz", "xy", None),
            P(("gz", "xy"), None),
            P(("gz", "xy")),
            P(("gz", "xy"), None),
        ),
        out_specs=(P("gz", "xy", None), P("gz", "xy", None)),
        check_vma=False,
    )
```

time: 1370 us -> 240 us (0.18); the launches traced: 1350 us -> 239 us
  local copies, waits for them, and re-layouts: 738 us -> 6.97 us
  other arithmetic: 304 us -> 3.55 us
  starting transfers between devices: 258 us -> 46.7 us
  Pallas kernels: 0 us -> 87.7 us
  waiting for transfers between devices: 41.2 us -> 79.5 us
    reshape x14 -> x0, local copies, waits for them, and re-layouts: 644 us -> none  [the longest x4 581 us: shrink(): values.reshape(zsize // 2, 2, xsize // 2, 2, ysize // 2, 2)]
    ppermute x84 -> x16, starting transfers between devices: 258 us -> 46.6 us  [both_ways(): return (lax.ppermute(to_high, axis, up), lax.ppermute(to_low, axis, down))]
    reduce_sum x6 -> x0, other arithmetic: 191 us -> none  [shrink(): values.reshape(zsize // 2, 2, xsize // 2, 2, ysize // 2, 2)]
    pallas_call x0 -> x7, Pallas kernels: none -> 87.7 us  [call(): pl.pallas_call(kernel, out_shape=tuple(outs), in_specs=[SMEM] * smem + [V...]
    add x17 -> x0, other arithmetic: 80.7 us -> none  [the longest x13 76 us: smooth_once(): values + OMEGA * (source - operate(values, diagonal, spread)) / diagonal]
    div x2 -> x0, local copies, waits for them, and re-layouts: 40.4 us -> none  [shrink(): values.reshape(zsize // 2, 2, xsize // 2, 2, ysize // 2, 2)]
    all_gather x0 -> x2, waiting for transfers between devices: none -> 27.4 us  [the longest x1 27.4 us: shards(): g2_all = lax.all_gather(g2, ('gz', 'xy'))]
    transpose x1 -> x0, local copies, waits for them, and re-layouts: 24 us -> none  [shards(): secretion = gathered.reshape(per_z, per_x, per_y, EDGE, EDGE, EDGE).trans...]
  transfers between devices with their start and end apart: 84 -> 18, of which waited for: 29 -> 7; matrix products, arithmetic and copies ran while one was open for 68% -> 3% of each run, Pallas kernels for 0% -> 21%
where the time goes in v1:
time: 240 us; the launch traced here: 239 us
  Pallas kernels  87.7 us (37%)
  waiting for transfers between devices  79.5 us (33%)
  starting transfers between devices  46.7 us (19%)
  between operations  14.4 us (6%)
  local copies, waits for them, and re-layouts  6.97 us (3%)
  other arithmetic  3.55 us (1%)
    pallas_call x7, Pallas kernels, call(): pl.pallas_call(kernel, out_shape=tuple(outs), in_specs=[SMEM] * smem + [V...  87.7 us
    ppermute x16, waiting for transfers between devices, both_ways(): return (lax.ppermute(to_high, axis, up), lax.ppermute(to_low, axis, down))  52.1 us
    ppermute x16, starting transfers between devices, both_ways(): return (lax.ppermute(to_high, axis, up), lax.ppermute(to_low, axis, down))  46.6 us
    all_gather x1, waiting for transfers between devices, shards(): g2_all = lax.all_gather(g2, ('gz', 'xy'))  27.4 us
  transfers between devices with their start and end apart: 18, of which 7 were waited for; matrix products, arithmetic and copies ran while one was open for 3% of the time, Pallas kernels for 21%

profile of v1, /device:TPU:0, one launch (start us, length us, event | category | flops | bytes accessed | tf_op | source)
XLA Modules:
  0.0 238.8 jit_solution(14740680435579152083)
XLA Ops:
  7.2 4.1 %shard_map.69 = (f32[16,16,512]{2,1,0:T(8,128)}, f32[64,256]{1,0:T(8,128)}) custom-call(f32[32,32,1024]{2,1,0:T(8,128)} %refs_2_.3), custom_call_target="tpu_custom_call" | custom-call | flops 95682560 | bytes 4784128 | tf_op jit(solution)/shard_map/pallas_call | solution.py:617
  11.3 4.5 %shard_map.68.refs_7_ = bf16[9,272,128]{2,1,0:T(8,128)(2,1)} custom-call(s32[72]{0:T(128)} %refs_0_.1, s32[1,9]{1,0:T(1,128)} %refs_1_.2, bf16[72,4096]{1,0:T(8,128)(2,1)} %refs_2_.2), custom_call_target="tpu_custom_call" | custom-call | flops 24336720 | bytes 1216836 | tf_op jit(solution)/shard_map/pallas_call | solution.py:617
  16.9 1.3 collective-permute-start.5
  18.2 3.0 %collective-permute-start.4 = (bf16[3,272,128]{2,1,0:T(8,128)(2,1)S(1)}, bf16[3,272,128]{2,1,0:T(8,128)(2,1)S(1)}, u32[]{:S(2)}, u32[]{:S(2)}) collective-permute-start(bf16[3,272,128]{2,1,0:T(8,128)(2,1)S(1)} %get-tuple-element.53), channel_id=1, source_target_pairs={{0,8},{8,16},{16,24},{1,9},{9,17},{17,25},{2,10},{10,18},{18,26},{... | collective-permute-start | bytes 626696 | tf_op jit(solution)/shard_map/ppermute | solution.py:636
  21.3 2.6 %convert.4 = bf16[32,32,1024]{2,1,0:T(8,128)(2,1)S(1)} convert(f32[32,32,1024]{2,1,0:T(8,128)} %refs_2_.3) | non-fusion elementwise | flops 1048576 | bytes 6291456 | tf_op jit(solution)/shard_map/convert.1
  23.8 1.3 collective-permute-start.1
  25.1 5.1 %collective-permute-start = (bf16[2,32,1024]{2,1,0:T(8,128)(2,1)S(1)}, bf16[2,32,1024]{2,1,0:T(8,128)(2,1)S(1)}, u32[]{:S(2)}, u32[]{:S(2)}) collective-permute-start(bf16[2,32,1024]{2,1,0:T(8,128)(2,1)S(1)} %get-tuple-element.49), channel_id=1, source_target_pairs={{0,8},{8,16},{16,24},{1,9},{9,17},{17,25},{2,10},{10,18},{18,26},{... | collective-permute-start | bytes 393224 | tf_op jit(solution)/shard_map/ppermute | solution.py:636
  30.2 1.8 fusion
  33.2 3.4 %collective-permute-start.2 = (f32[36,2,1024]{2,1,0:T(2,128)S(1)}, f32[36,2,1024]{2,1,0:T(2,128)S(1)}, u32[]{:S(2)}, u32[]{:S(2)}) collective-permute-start(f32[36,2,1024]{2,1,0:T(2,128)S(1)} %pad_maximum_fusion), channel_id=1, source_target_pairs={{0,1},{1,2},{2,3},{3,4},{4,5},{5,6},{6,7},{8,9},{9,10},{10,11},{11... | collective-permute-start | bytes 884744 | tf_op jit(solution)/shard_map/ppermute | solution.py:636
  36.7 1.3 collective-permute-start.3
  38.1 4.6 %collective-permute-start.6 = (bf16[3,272,128]{2,1,0:T(8,128)(2,1)S(1)}, bf16[3,272,128]{2,1,0:T(8,128)(2,1)S(1)}, u32[]{:S(2)}, u32[]{:S(2)}) collective-permute-start(bf16[3,272,128]{2,1,0:T(8,128)(2,1)S(1)} %pad_maximum_fusion.2), channel_id=1, source_target_pairs={{0,1},{1,2},{2,3},{3,4},{4,5},{5,6},{6,7},{8,9},{9,10},{10,11},{11... | collective-permute-start | bytes 626696 | tf_op jit(solution)/shard_map/ppermute | solution.py:636
  42.8 1.3 collective-permute-start.7
  44.7 15.6 %collective-permute-done.6.refs_10_ = bf16[3,272,128]{2,1,0:T(8,128)(2,1)S(1)} collective-permute-done((bf16[3,272,128]{2,1,0:T(8,128)(2,1)S(1)}, bf16[3,272,128]{2,1,0:T(8,128)(2,1)S(1)}, u32[]{:S(2)}, u32[]{:S(2)}) %collective-permute-start.6) | collective-permute-done | bytes 208928 | tf_op jit(solution)/shard_map/ppermute | solution.py:636
  61.4 31.9 %shard_map.70 = (f32[32,32,1024]{2,1,0:T(8,128)}, f32[20,24,512]{2,1,0:T(8,128)}, bf16[240,512]{1,0:T(8,128)(2,1)}, bf16[240,512]{1,0:T(8,128)(2,1)}, bf16[200,1...) custom-call(s32[2]{0:T(128)} %pad_add_fusion.refs_0_, ...), custom_call_target="tpu_custom_call" | custom-call | flops 613826688 | bytes 30691336 | tf_op jit(solution)/shard_map/pallas_call | solution.py:617
  93.2 2.8 %collective-permute-start.8 = (bf16[240,512]{1,0:T(8,128)(2,1)}, bf16[240,512]{1,0:T(8,128)(2,1)S(1)}, u32[]{:S(2)}, u32[]{:S(2)}) collective-permute-start(bf16[240,512]{1,0:T(8,128)(2,1)} %get-tuple-element.27), channel_id=1, source_target_pairs={{0,8},{8,16},{16,24},{1,9},{9,17},{17,25},{2,10},{10,18},{18,26},{... | collective-permute-start | bytes 737288 | tf_op jit(solution)/shard_map/ppermute | solution.py:636
  96.0 1.3 collective-permute-start.9
  97.3 2.3 collective-permute-done.9.mzh
  100.3 3.2 %shard_map.71 = (f32[24,24,512]{2,1,0:T(8,128)}, f32[24,24,512]{2,1,0:T(8,128)}, bf16[384,512]{1,0:T(8,128)(2,1)}, bf16[384,512]{1,0:T(8,128)(2,1)}) custom-call(f32[20,24,512]{2,1,0:T(8,128)} %get-tuple-element.26.c1, f32[16,16,512]{2,1,0:T(8,128)} %get-tuple-element.24.refs_12_.r1, bf16[240,512]{1,0:T(8,128)(2,1)} %copy-done.10, bf16[240,512]{1,0:T(8,128)(2,1)} %copy-done.11), custom_call_target="tpu_custom_call" | custom-call | flops 102891520 | bytes 5144576 | tf_op jit(solution)/shard_map/pallas_call | solution.py:617
  103.5 4.2 %collective-permute-start.10 = (bf16[384,512]{1,0:T(8,128)(2,1)}, bf16[384,512]{1,0:T(8,128)(2,1)S(1)}, u32[]{:S(2)}, u32[]{:S(2)}) collective-permute-start(bf16[384,512]{1,0:T(8,128)(2,1)} %get-tuple-element.31), channel_id=1, source_target_pairs={{0,1},{1,2},{2,3},{3,4},{4,5},{5,6},{6,7},{8,9},{9,10},{10,11},{11... | collective-permute-start | bytes 1179656 | tf_op jit(solution)/shard_map/ppermute | solution.py:636
  107.8 1.3 collective-permute-start.11
  109.1 5.0 %collective-permute-done.10.refs_3_ = bf16[384,512]{1,0:T(8,128)(2,1)S(1)} collective-permute-done((bf16[384,512]{1,0:T(8,128)(2,1)}, bf16[384,512]{1,0:T(8,128)(2,1)S(1)}, u32[]{:S(2)}, u32[]{:S(2)}) %collective-permute-start.10) | collective-permute-done | bytes 393248 | tf_op jit(solution)/shard_map/ppermute | solution.py:636
  114.1 5.1 %collective-permute-done.11.refs_4_ = bf16[384,512]{1,0:T(8,128)(2,1)S(1)} collective-permute-done((bf16[384,512]{1,0:T(8,128)(2,1)}, bf16[384,512]{1,0:T(8,128)(2,1)S(1)}, u32[]{:S(2)}, u32[]{:S(2)}) %collective-permute-start.11) | collective-permute-done | bytes 393248 | tf_op jit(solution)/shard_map/ppermute | solution.py:636
  120.0 7.5 %shard_map.72 = (f32[24,24,512]{2,1,0:T(8,128)}, f32[24,24,512]{2,1,0:T(8,128)}, f32[24,24,512]{2,1,0:T(8,128)}, f32[64,256]{1,0:T(8,128)}) custom-call(s32[2]{0:T(128)} %pad_add_fusion.refs_0_, f32[24,24,512]{2,1,0:T(8,128)} %get-tuple-element.29.refs_1_, f32[24,24,512]{2,1,0:T(8,128)} %get-tuple-element.30.refs_2_, bf16[384,512]{1,0:T(8,128)(2,1)} %copy-done.6, ...), custom_call_target="tpu_custom_call" | custom-call | flops 135004320 | bytes 6750216 | tf_op jit(solution)/shard_map/pallas_call | solution.py:617
  127.5 9.0 %collective-permute-start.12 = (bf16[200,1024]{1,0:T(8,128)(2,1)S(1)}, bf16[200,1024]{1,0:T(8,128)(2,1)S(1)}, u32[]{:S(2)}, u32[]{:S(2)}) collective-permute-start(bf16[200,1024]{1,0:T(8,128)(2,1)S(1)} %copy-done.17), channel_id=1, source_target_pairs={{0,8},{8,16},{16,24},{1,9},{9,17},{17,25},{2,10},{10,18},{18,26},{... | collective-permute-start | bytes 1228808 | tf_op jit(solution)/shard_map/ppermute | solution.py:636
  136.5 1.3 collective-permute-start.13
  137.8 2.3 collective-permute-done.13.vzh.refs_5_
  140.9 2.6 %shard_map.73 = (bf16[288,1024]{1,0:T(8,128)(2,1)}, bf16[288,1024]{1,0:T(8,128)(2,1)}) custom-call(bf16[288,1024]{1,0:T(8,128)(2,1)} %get-tuple-element.38.pxl, bf16[288,1024]{1,0:T(8,128)(2,1)} %get-tuple-element.39.pxh, bf16[200,1024]{1,0:T(8,128)(2,1)} %copy-done, bf16[200,1024]{1,0:T(8,128)(2,1)} %copy-done.1), custom_call_target="tpu_custom_call" | custom-call | flops 63569920 | bytes 3178496 | tf_op jit(solution)/shard_map/pallas_call | solution.py:617
  143.4 4.0 %collective-permute-start.14 = (bf16[288,1024]{1,0:T(8,128)(2,1)}, bf16[288,1024]{1,0:T(8,128)(2,1)S(1)}, u32[]{:S(2)}, u32[]{:S(2)}) collective-permute-start(bf16[288,1024]{1,0:T(8,128)(2,1)} %get-tuple-element.40), channel_id=1, source_target_pairs={{0,1},{1,2},{2,3},{3,4},{4,5},{5,6},{6,7},{8,9},{9,10},{10,11},{11... | collective-permute-start | bytes 1769480 | tf_op jit(solution)/shard_map/ppermute | solution.py:636
  147.5 1.5 collective-permute-start.15
  148.9 21.6 %collective-permute-done.14.refs_6_ = bf16[288,1024]{1,0:T(8,128)(2,1)S(1)} collective-permute-done((bf16[288,1024]{1,0:T(8,128)(2,1)}, bf16[288,1024]{1,0:T(8,128)(2,1)S(1)}, u32[]{:S(2)}, u32[]{:S(2)}) %collective-permute-start.14) | collective-permute-done | bytes 589856 | tf_op jit(solution)/shard_map/ppermute | solution.py:636
  170.6 27.4 %all-gather.5.cloned.1.call-done = f32[2048,256]{1,0:T(8,128)} async-done(((f32[64,256]{1,0:T(8,128)}), f32[2048,256]{1,0:T(8,128)}) %all-gather.5.cloned.1.call-update) | async-done | bytes 2097168 | tf_op jit(solution)/shard_map/all_gather | solution.py:718
  198.0 34.0 %shard_map.74 = f32[32,32,1024]{2,1,0:T(8,128)} custom-call(s32[2]{0:T(128)} %pad_add_fusion.refs_0_, f32[24,24,512]{2,1,0:T(8,128)} %get-tuple-element.33.refs_1_, f32[24,24,512]{2,1,0:T(8,128)} %get-tuple-element.34.refs_2_, f32[24,24,512]{2,1,0:T(8,128)} %get-tuple-element.35.refs_3_, bf16[200,1024]{1,0:T(8,128)(2,1)} %copy-done, ...), custom_call_target="tpu_custom_call" | custom-call | flops 598343808 | bytes 29917192 | tf_op jit(solution)/shard_map/pallas_call | solution.py:617
  (63 shorter events, 6.4 us)
Async XLA Ops:
  7.2 163.4 %all-gather.7.cloned.1.call-start = ((), (), s32[]{:S(2)}) async-start(), calls=%async_computation.1 | async-start | bytes 2162688 | tf_op jit(solution)/shard_map/all_gather | solution.py:660
  11.3 186.7 %all-gather.5.cloned.1.call-start = ((), (), s32[]{:S(2)}) async-start(), calls=%async_computation | async-start | bytes 2162688 | tf_op jit(solution)/shard_map/all_gather | solution.py:718
  16.9 21.1 %collective-permute-start.5 = (bf16[3,272,128]{2,1,0:T(8,128)(2,1)S(1)}, bf16[3,272,128]{2,1,0:T(8,128)(2,1)S(1)}, u32[]{:S(2)}, u32[]{:S(2)}) collective-permute-start(bf16[3,272,128]{2,1,0:T(8,128)(2,1)S(1)} %get-tuple-element.52), channel_id=1, source_target_pairs={{8,0},{16,8},{24,16},{9,1},{17,9},{25,17},{10,2},{18,10},{26,18},{... | collective-permute-start | bytes 626696 | tf_op jit(solution)/shard_map/ppermute | solution.py:636
  18.2 19.9 %collective-permute-start.4 = (bf16[3,272,128]{2,1,0:T(8,128)(2,1)S(1)}, bf16[3,272,128]{2,1,0:T(8,128)(2,1)S(1)}, u32[]{:S(2)}, u32[]{:S(2)}) collective-permute-start(bf16[3,272,128]{2,1,0:T(8,128)(2,1)S(1)} %get-tuple-element.53), channel_id=1, source_target_pairs={{0,8},{8,16},{16,24},{1,9},{9,17},{17,25},{2,10},{10,18},{18,26},{... | collective-permute-start | bytes 626696 | tf_op jit(solution)/shard_map/ppermute | solution.py:636
  23.8 9.1 %collective-permute-start.1 = (bf16[2,32,1024]{2,1,0:T(8,128)(2,1)S(1)}, bf16[2,32,1024]{2,1,0:T(8,128)(2,1)S(1)}, u32[]{:S(2)}, u32[]{:S(2)}) collective-permute-start(bf16[2,32,1024]{2,1,0:T(8,128)(2,1)S(1)} %get-tuple-element.48), channel_id=1, source_target_pairs={{8,0},{16,8},{24,16},{9,1},{17,9},{25,17},{10,2},{18,10},{26,18},{... | collective-permute-start | bytes 393224 | tf_op jit(solution)/shard_map/ppermute | solution.py:636
  25.1 7.8 %collective-permute-start = (bf16[2,32,1024]{2,1,0:T(8,128)(2,1)S(1)}, bf16[2,32,1024]{2,1,0:T(8,128)(2,1)S(1)}, u32[]{:S(2)}, u32[]{:S(2)}) collective-permute-start(bf16[2,32,1024]{2,1,0:T(8,128)(2,1)S(1)} %get-tuple-element.49), channel_id=1, source_target_pairs={{0,8},{8,16},{16,24},{1,9},{9,17},{17,25},{2,10},{10,18},{18,26},{... | collective-permute-start | bytes 393224 | tf_op jit(solution)/shard_map/ppermute | solution.py:636
  32.9 27.4 %copy-start.14 = (bf16[2,32,1024]{2,1,0:T(8,128)(2,1)}, bf16[2,32,1024]{2,1,0:T(8,128)(2,1)S(1)}, u32[]{:S(2)}) copy-start(bf16[2,32,1024]{2,1,0:T(8,128)(2,1)S(1)} %collective-permute-done.1.refs_4_) | copy-start | bytes 393220
  33.0 27.4 %copy-start.15 = (bf16[2,32,1024]{2,1,0:T(8,128)(2,1)}, bf16[2,32,1024]{2,1,0:T(8,128)(2,1)S(1)}, u32[]{:S(2)}) copy-start(bf16[2,32,1024]{2,1,0:T(8,128)(2,1)S(1)} %collective-permute-done.refs_3_) | copy-start | bytes 393220
  33.2 27.2 %collective-permute-start.2 = (f32[36,2,1024]{2,1,0:T(2,128)S(1)}, f32[36,2,1024]{2,1,0:T(2,128)S(1)}, u32[]{:S(2)}, u32[]{:S(2)}) collective-permute-start(f32[36,2,1024]{2,1,0:T(2,128)S(1)} %pad_maximum_fusion), channel_id=1, source_target_pairs={{0,1},{1,2},{2,3},{3,4},{4,5},{5,6},{6,7},{8,9},{9,10},{10,11},{11... | collective-permute-start | bytes 884744 | tf_op jit(solution)/shard_map/ppermute | solution.py:636
  36.7 23.7 %collective-permute-start.3 = (f32[36,2,1024]{2,1,0:T(2,128)S(1)}, f32[36,2,1024]{2,1,0:T(2,128)S(1)}, u32[]{:S(2)}, u32[]{:S(2)}) collective-permute-start(f32[36,2,1024]{2,1,0:T(2,128)S(1)} %pad_maximum_fusion.1), channel_id=1, source_target_pairs={{1,0},{2,1},{3,2},{4,3},{5,4},{6,5},{7,6},{9,8},{10,9},{11,10},{12... | collective-permute-start | bytes 884744 | tf_op jit(solution)/shard_map/ppermute | solution.py:636
  38.0 22.4 %copy-start.4 = (bf16[3,272,128]{2,1,0:T(8,128)(2,1)}, bf16[3,272,128]{2,1,0:T(8,128)(2,1)S(1)}, u32[]{:S(2)}) copy-start(bf16[3,272,128]{2,1,0:T(8,128)(2,1)S(1)} %collective-permute-done.5.refs_9_) | copy-start | bytes 626692
  38.1 22.4 %copy-start.5 = (bf16[3,272,128]{2,1,0:T(8,128)(2,1)}, bf16[3,272,128]{2,1,0:T(8,128)(2,1)S(1)}, u32[]{:S(2)}) copy-start(bf16[3,272,128]{2,1,0:T(8,128)(2,1)S(1)} %collective-permute-done.4.refs_8_) | copy-start | bytes 626692
  38.1 22.2 %collective-permute-start.6 = (bf16[3,272,128]{2,1,0:T(8,128)(2,1)S(1)}, bf16[3,272,128]{2,1,0:T(8,128)(2,1)S(1)}, u32[]{:S(2)}, u32[]{:S(2)}) collective-permute-start(bf16[3,272,128]{2,1,0:T(8,128)(2,1)S(1)} %pad_maximum_fusion.2), channel_id=1, source_target_pairs={{0,1},{1,2},{2,3},{3,4},{4,5},{5,6},{6,7},{8,9},{9,10},{10,11},{11... | collective-permute-start | bytes 626696 | tf_op jit(solution)/shard_map/ppermute | solution.py:636
  42.8 17.6 %collective-permute-start.7 = (bf16[3,272,128]{2,1,0:T(8,128)(2,1)S(1)}, bf16[3,272,128]{2,1,0:T(8,128)(2,1)S(1)}, u32[]{:S(2)}, u32[]{:S(2)}) collective-permute-start(bf16[3,272,128]{2,1,0:T(8,128)(2,1)S(1)} %pad_maximum_fusion.3), channel_id=1, source_target_pairs={{1,0},{2,1},{3,2},{4,3},{5,4},{6,5},{7,6},{9,8},{10,9},{11,10},{12... | collective-permute-start | bytes 626696 | tf_op jit(solution)/shard_map/ppermute | solution.py:636
  60.4 0.8 copy-start.13
  60.4 0.9 copy-start.8
  60.4 1.0 copy-start.9
  93.2 4.1 %collective-permute-start.8 = (bf16[240,512]{1,0:T(8,128)(2,1)}, bf16[240,512]{1,0:T(8,128)(2,1)S(1)}, u32[]{:S(2)}, u32[]{:S(2)}) collective-permute-start(bf16[240,512]{1,0:T(8,128)(2,1)} %get-tuple-element.27), channel_id=1, source_target_pairs={{0,8},{8,16},{16,24},{1,9},{9,17},{17,25},{2,10},{10,18},{18,26},{... | collective-permute-start | bytes 737288 | tf_op jit(solution)/shard_map/ppermute | solution.py:636
  96.0 3.6 %collective-permute-start.9 = (bf16[240,512]{1,0:T(8,128)(2,1)}, bf16[240,512]{1,0:T(8,128)(2,1)S(1)}, u32[]{:S(2)}, u32[]{:S(2)}) collective-permute-start(bf16[240,512]{1,0:T(8,128)(2,1)} %get-tuple-element.28), channel_id=1, source_target_pairs={{8,0},{16,8},{24,16},{9,1},{17,9},{25,17},{10,2},{18,10},{26,18},{... | collective-permute-start | bytes 737288 | tf_op jit(solution)/shard_map/ppermute | solution.py:636
  97.3 2.3 copy-start.10
  103.5 23.9 %copy-start.17 = (bf16[200,1024]{1,0:T(8,128)(2,1)S(1)}, bf16[200,1024]{1,0:T(8,128)(2,1)}, u32[]{:S(2)}) copy-start(bf16[200,1024]{1,0:T(8,128)(2,1)} %get-tuple-element.36) | copy-start | bytes 1228804
  103.5 32.9 %copy-start.16 = (bf16[200,1024]{1,0:T(8,128)(2,1)S(1)}, bf16[200,1024]{1,0:T(8,128)(2,1)}, u32[]{:S(2)}) copy-start(bf16[200,1024]{1,0:T(8,128)(2,1)} %get-tuple-element.37) | copy-start | bytes 1228804
  103.5 10.6 %collective-permute-start.10 = (bf16[384,512]{1,0:T(8,128)(2,1)}, bf16[384,512]{1,0:T(8,128)(2,1)S(1)}, u32[]{:S(2)}, u32[]{:S(2)}) collective-permute-start(bf16[384,512]{1,0:T(8,128)(2,1)} %get-tuple-element.31), channel_id=1, source_target_pairs={{0,1},{1,2},{2,3},{3,4},{4,5},{5,6},{6,7},{8,9},{9,10},{10,11},{11... | collective-permute-start | bytes 1179656 | tf_op jit(solution)/shard_map/ppermute | solution.py:636
  107.8 11.5 %collective-permute-start.11 = (bf16[384,512]{1,0:T(8,128)(2,1)}, bf16[384,512]{1,0:T(8,128)(2,1)S(1)}, u32[]{:S(2)}, u32[]{:S(2)}) collective-permute-start(bf16[384,512]{1,0:T(8,128)(2,1)} %get-tuple-element.32), channel_id=1, source_target_pairs={{1,0},{2,1},{3,2},{4,3},{5,4},{6,5},{7,6},{9,8},{10,9},{11,10},{12... | collective-permute-start | bytes 1179656 | tf_op jit(solution)/shard_map/ppermute | solution.py:636
  114.1 5.2 %copy-start.6 = (bf16[384,512]{1,0:T(8,128)(2,1)}, bf16[384,512]{1,0:T(8,128)(2,1)S(1)}, u32[]{:S(2)}) copy-start(bf16[384,512]{1,0:T(8,128)(2,1)S(1)} %collective-permute-done.10.refs_3_) | copy-start | bytes 1179652
  127.5 10.3 %collective-permute-start.12 = (bf16[200,1024]{1,0:T(8,128)(2,1)S(1)}, bf16[200,1024]{1,0:T(8,128)(2,1)S(1)}, u32[]{:S(2)}, u32[]{:S(2)}) collective-permute-start(bf16[200,1024]{1,0:T(8,128)(2,1)S(1)} %copy-done.17), channel_id=1, source_target_pairs={{0,8},{8,16},{16,24},{1,9},{9,17},{17,25},{2,10},{10,18},{18,26},{... | collective-permute-start | bytes 1228808 | tf_op jit(solution)/shard_map/ppermute | solution.py:636
  136.5 3.6 %collective-permute-start.13 = (bf16[200,1024]{1,0:T(8,128)(2,1)S(1)}, bf16[200,1024]{1,0:T(8,128)(2,1)S(1)}, u32[]{:S(2)}, u32[]{:S(2)}) collective-permute-start(bf16[200,1024]{1,0:T(8,128)(2,1)S(1)} %copy-done.16), channel_id=1, source_target_pairs={{8,0},{16,8},{24,16},{9,1},{17,9},{25,17},{10,2},{18,10},{26,18},{... | collective-permute-start | bytes 1228808 | tf_op jit(solution)/shard_map/ppermute | solution.py:636
  137.8 2.3 copy-start
  143.4 27.1 %collective-permute-start.14 = (bf16[288,1024]{1,0:T(8,128)(2,1)}, bf16[288,1024]{1,0:T(8,128)(2,1)S(1)}, u32[]{:S(2)}, u32[]{:S(2)}) collective-permute-start(bf16[288,1024]{1,0:T(8,128)(2,1)} %get-tuple-element.40), channel_id=1, source_target_pairs={{0,1},{1,2},{2,3},{3,4},{4,5},{5,6},{6,7},{8,9},{9,10},{10,11},{11... | collective-permute-start | bytes 1769480 | tf_op jit(solution)/shard_map/ppermute | solution.py:636
  147.5 23.1 %collective-permute-start.15 = (bf16[288,1024]{1,0:T(8,128)(2,1)}, bf16[288,1024]{1,0:T(8,128)(2,1)S(1)}, u32[]{:S(2)}, u32[]{:S(2)}) collective-permute-start(bf16[288,1024]{1,0:T(8,128)(2,1)} %get-tuple-element.41), channel_id=1, source_target_pairs={{1,0},{2,1},{3,2},{4,3},{5,4},{6,5},{7,6},{9,8},{10,9},{11,10},{12... | collective-permute-start | bytes 1769480 | tf_op jit(solution)/shard_map/ppermute | solution.py:636
  170.6 27.4 %copy-start.2 = (bf16[288,1024]{1,0:T(8,128)(2,1)}, bf16[288,1024]{1,0:T(8,128)(2,1)S(1)}, u32[]{:S(2)}) copy-start(bf16[288,1024]{1,0:T(8,128)(2,1)S(1)} %collective-permute-done.14.refs_6_) | copy-start | bytes 1769476
  170.6 27.4 %copy-start.3 = (bf16[288,1024]{1,0:T(8,128)(2,1)}, bf16[288,1024]{1,0:T(8,128)(2,1)S(1)}, u32[]{:S(2)}) copy-start(bf16[288,1024]{1,0:T(8,128)(2,1)S(1)} %collective-permute-done.15.refs_7_) | copy-start | bytes 1769476
  (4 other events, 2.9 us)
Sparse Core Ops, SparseCore 0:
  11.4 68.0 all-gather.6
  127.6 70.3 all-gather.4

commit v2 on v1

--- a/solution.py
+++ b/solution.py
@@ -134,7 +134,7 @@
     loop(0, 9, block)
 
 
-def rates_kernel(uptake, r1, r2, rs, xp, rs1, xp1):
+def rates_kernel(uptake, r1, r2, zl, zh, z2l, z2h, xl, xh, rs, xp, rs1, xp1):
     def pair(m):
         for t in range(NT):
             both = uptake[2 * m, :, lanes(t)] + uptake[2 * m + 1, :, lanes(t)]
@@ -150,14 +150,115 @@
             xp1[t, m] = halve_rows(both, rs1, t)
 
     loop(0, 8, pair1)
+    coarse = []
     for t, tile in enumerate(halve_lanes(xp1, 8, 8)):
         r2[:, lanes(t)] = tile.reshape(64, 128)
+        coarse.append(tile.reshape(64, 128).astype(BF16))
+    z2l[...] = r2[0:32, :].astype(BF16)
+    z2h[...] = r2[32:64, :].astype(BF16)
+    for ref, u, r in ((zl, slice(0, 2), slice(0, 4)), (zh, slice(30, 32), slice(12, 16))):
+        ref[0:64, :] = uptake[u].reshape(64, 1024).astype(BF16)
+        ref[64:128, 0:512] = r1[r].reshape(64, 512).astype(BF16)
+        for t in range(2):
+            ref[64:128, lanes(4 + t)] = coarse[t]
+        ref[64:128, 768:1024] = jnp.zeros((64, 256), BF16)
+
+    sub = iota((8, 1024), 0)
+
+    def columns(i):
+        lows, highs = [], []
+        for j in range(2):
+            low, high = jnp.zeros((8, 1024), F32), jnp.zeros((8, 1024), F32)
+            for n in range(4):
+                z = 8 * i + 4 * j + n
+                low = jnp.where(sub // 2 == n, shifted(uptake[z, 0:8, :], 2 * n, 0), low)
+                high = jnp.where(sub // 2 == n, shifted(uptake[z, 24:32, :], 2 * n + 2, 0), high)
+            lows.append(low)
+            highs.append(high)
+        rows = pl.ds(pl.multiple_of(16 * i, 16), 16)
+        xl[rows, :] = jnp.concatenate(lows, axis=0).astype(BF16)
+        xh[rows, :] = jnp.concatenate(highs, axis=0).astype(BF16)
+
+    loop(0, 4, columns)
+
+
+def halves(sub, first, second):
+    return jnp.where(sub < 4, first, shifted(second, 4, 1))
+
+
+def uppers(sub, first, second):
+    return jnp.where(sub < 4, shifted(first, 4, 1), second)
+
+
+def far_messages(window):
+    planes, _, width = window.shape
+    pairs = window.reshape(planes // 2, 2, 8, width)
+    sub = iota((planes // 2, 8, width), 1)
+    size = (planes * 4, width)
+    return halves(sub, pairs[:, 0], pairs[:, 1]).reshape(size), uppers(sub, pairs[:, 0], pairs[:, 1]).reshape(size)
+
+
+def far_tile(from_low, from_high):
+    width = from_low.shape[-1]
+    low, high = from_low.reshape(-1, 8, width), from_high.reshape(-1, 8, width)
+    sub = iota(low.shape, 1)
+    even = jnp.where(sub < 4, high, shifted(low, 4, 1))
+    odd = jnp.where(sub < 4, shifted(high, 4, 1), low)
+    return jnp.stack([even, odd], axis=1).reshape(-1, 8, width)
+
+
+def rates_window_kernel(r1, r2, xl, xh, zl, zh, z2l, z2h, q1, q2, ul, uh, cl, ch, fl, fh):
+    low, high = zl[...].astype(F32), zh[...].astype(F32)
+    sub = iota((8, 1024), 0)
+    ul[0:64, :] = xl[...]
+    uh[0:64, :] = xh[...]
+    planes = [low[0:32], low[32:64], high[0:32], high[32:64]]
+    to_low, to_high = jnp.zeros((8, 1024), F32), jnp.zeros((8, 1024), F32)
+    for n, p in enumerate(planes):
+        to_low = jnp.where(sub // 2 == n, shifted(p[0:8], 2 * n, 0), to_low)
+        to_high = jnp.where(sub // 2 == n, shifted(p[24:32], 2 * n + 2, 0), to_high)
+    blank = jnp.zeros((8, 1024), F32)
+    ul[64:80, :] = jnp.concatenate([to_low, blank], axis=0).astype(BF16)
+    uh[64:80, :] = jnp.concatenate([to_high, blank], axis=0).astype(BF16)
+
+    q1[0:4, 0:16, :] = low[64:128, 0:512].reshape(4, 16, 512)
+    q1[4:20, 0:16, :] = r1[...]
+    q1[20:24, 0:16, :] = high[64:128, 0:512].reshape(4, 16, 512)
+    q1[:, 16:24, :] = jnp.zeros((24, 8, 512), F32)
+    sub1 = iota((12, 8, 512), 1)
+    first = q1[:, 0:8, :].reshape(12, 2, 8, 512)
+    last = q1[:, 8:16, :].reshape(12, 2, 8, 512)
+    cl[0:96, :] = halves(sub1, first[:, 0], first[:, 1]).reshape(96, 512).astype(BF16)
+    ch[0:96, :] = uppers(sub1, last[:, 0], last[:, 1]).reshape(96, 512).astype(BF16)
+
+    window = window_planes(r2[...], low[64:128, 512:768], high[64:128, 512:768], z2l[...].astype(F32), z2h[...].astype(F32))
+    q2[...] = window
+    for ref in (cl, ch):
+        ref[96:224, 0:256] = window[0:16].reshape(128, 256).astype(BF16)
+        ref[96:224, 256:512] = window[16:32].reshape(128, 256).astype(BF16)
+    to_low, to_high = far_messages(window)
+    fl[...] = to_low.astype(BF16)
+    fh[...] = to_high.astype(BF16)
+
+
+def window_planes(own, low, high, low2, high2):
+    parts = (low2, low, own, high, high2)
+    return jnp.concatenate([a.reshape(-1, 8, 256) for a in parts], axis=0)
+
+
+def source_window_kernel(own, low, high, low2, high2, window, near, fl, fh):
+    planes = window_planes(own[...], low[...], high[...], low2[...], high2[...])
+    window[...] = planes
+    near[...] = planes.reshape(256, 256).astype(BF16)
+    to_low, to_high = far_messages(planes)
+    fl[...] = to_low.astype(BF16)
+    fh[...] = to_high.astype(BF16)
 
 
 def pre_kernel(
-    nz, nx, info, density, uptake, uzl, uzh, uxl, uxr, own, zl, zh, xl, xr, r1,
+    nz, nx, info, density, uptake, uz_low, uz_high, ux_low, ux_high, own, zl, zh, xl, xr,
     supply, c1, mzl, mzh, vzl, vzh, pxl, pxh, v_out, g_out,
-    va, vb, dd, gg, hot, rs, xp, sems,
+    va, vb, dd, gg, hot, rs, xp, usl, ush, sems,
 ):
     iz, ix = info[0], info[1]
     k = spread(0)
@@ -172,27 +273,34 @@
 
     sub8 = iota((8, 1024), 0)
 
-    def set_plane(q, rates, valid_z):
+    usl[...] = ux_low[...].astype(F32)
+    ush[...] = ux_high[...].astype(F32)
+
+    def set_plane(q, rates, low, high, valid_z):
         gz = jnp.where(valid_z, OMEGA, 0.0)
         d = rates + base
         dd[q, 0:32, :] = d
         gg[q, 0:32, :] = gz / d
-        high = jnp.concatenate([uxr[q], jnp.zeros((6, 1024), F32)], axis=0)
-        low = jnp.concatenate([jnp.zeros((6, 1024), F32), uxl[q]], axis=0)
-        d = high + low + base
+        d = jnp.where(sub8 < 2, high, jnp.where(sub8 >= 6, low, 0.0)) + base
         dd[q, 32:40, :] = d
         omega = jnp.where(sub8 < 2, jnp.where(ix < nx - 1, gz, 0.0), jnp.where(sub8 >= 6, jnp.where(ix > 0, gz, 0.0), 0.0))
         gg[q, 32:40, :] = omega / d
 
-    def own_plane(z):
-        va[z + O, 0:32, :] = density[z]
-        va[z + O, 32:40, :] = jnp.zeros((8, 1024), F32)
-        set_plane(z + Q, uptake[z], True)
-
-    loop(0, C, own_plane)
-    for i in range(2):
-        set_plane(i, uzl[i].astype(F32), iz > 0)
-        set_plane(34 + i, uzh[i].astype(F32), iz < nz - 1)
+    def own_planes(i):
+        rows = pl.ds(pl.multiple_of(8 * i, 8), 8)
+        low, high = usl[rows, :], ush[rows, :]
+        for n in range(4):
+            z = 4 * i + n
+            va[z + O, 0:32, :] = density[z]
+            va[z + O, 32:40, :] = jnp.zeros((8, 1024), F32)
+            set_plane(z + Q, uptake[z], shifted(low, 6 - 2 * n, 0), shifted(high, -2 * n, 0), True)
+
+    loop(0, C // 4, own_planes)
+    low, high = usl[64:72, :], ush[64:72, :]
+    for n in range(4):
+        rates = (uz_low if n < 2 else uz_high)[0:64, :].astype(F32)[32 * (n % 2) : 32 * (n % 2) + 32]
+        exists = iz > 0 if n < 2 else iz < nz - 1
+        set_plane(n if n < 2 else 32 + n, rates, shifted(low, 6 - 2 * n, 0), shifted(high, -2 * n, 0), exists)
 
     blocks = [own.at[4], zl.at[1], zh.at[1]] + [xl.at[i] for i in range(3)] + [xr.at[i] for i in range(3)]
     lane = iota((1, 128), 1)
@@ -278,11 +386,8 @@
         c1[:, 0:16, lanes(t)] = tile[:, 0:16]
         c1[:, 16:24, lanes(t)] = last
 
-    blank = jnp.zeros((4, 8, 512), F32)
-    low = jnp.concatenate([c1[0:6], jnp.concatenate([r1[0:4], blank], axis=1)], axis=0)
-    mzl[...] = low.reshape(240, 512).astype(BF16)
-    high = jnp.concatenate([c1[14:20], jnp.concatenate([r1[12:16], blank], axis=1)], axis=0)
-    mzh[...] = high.reshape(240, 512).astype(BF16)
+    mzl[...] = c1[0:6].reshape(144, 512).astype(BF16)
+    mzh[...] = c1[14:20].reshape(144, 512).astype(BF16)
 
     empty = jnp.zeros((1, 8, 1024), F32)
     low = jnp.concatenate([va[3:7], jnp.concatenate([supply[0:1], empty], axis=1)], axis=0)
@@ -293,87 +398,120 @@
     def sides(i):
         lows, highs = [], []
         for j in range(2):
-            p = 2 * i + j
-            z = p - 2
-            held = jnp.where((z >= 0) & (z < C), 1.0, 0.0)
-            zc = jnp.clip(z, 0, C - 1)
-            f_low = shifted(supply[zc, 0:8, :], 4, 0) * held
-            f_high = shifted(supply[zc, 24:32, :], 5, 0) * held
-            first, last, halo = va[p + 3, 0:8, :], va[p + 3, 24:32, :], va[p + 3, 32:40, :]
-            lows.append(pack_low(sub8, first, halo, f_low))
-            highs.append(pack_high(sub8, last, halo, f_high))
+            p = 4 * i + 2 * j + 3
+            lows.append(pack_low(va[p], va[p + 1]))
+            highs.append(pack_high(va[p], va[p + 1]))
         rows = pl.ds(pl.multiple_of(16 * i, 16), 16)
         pxl[rows, :] = jnp.concatenate(lows, axis=0).astype(BF16)
         pxh[rows, :] = jnp.concatenate(highs, axis=0).astype(BF16)
 
-    loop(0, 18, sides)
+    loop(0, 9, sides)
+
+    def sources(i):
+        lows, highs = [], []
+        for j in range(2):
+            low, high = jnp.zeros((8, 1024), F32), jnp.zeros((8, 1024), F32)
+            for n in range(8):
+                z = 16 * i + 8 * j + n
+                low = jnp.where(sub8 == n, shifted(supply[z, 0:8, :], n, 0), low)
+                high = jnp.where(sub8 == n, shifted(supply[z, 24:32, :], n + 1, 0), high)
+            lows.append(low)
+            highs.append(high)
+        rows = pl.ds(pl.multiple_of(16 * i + 144, 16), 16)
+        pxl[rows, :] = jnp.concatenate(lows, axis=0).astype(BF16)
+        pxh[rows, :] = jnp.concatenate(highs, axis=0).astype(BF16)
+
+    loop(0, 2, sources)
     v_copy.wait()
     g_copy.wait()
 
 
-def pack_low(sub, first, halo, f):
-    return jnp.where(sub < 2, first, jnp.where(sub >= 6, halo, jnp.where(sub == 4, f, 0.0)))
-
-
-def pack_high(sub, last, halo, f):
-    return jnp.where(sub >= 6, last, jnp.where(sub < 2, halo, jnp.where(sub == 4, f, 0.0)))
+def outer_rows(sub):
+    return (sub < 2) | (sub >= 6)
+
+
+def pack_pair(sub, a, b):
+    return jnp.where(outer_rows(sub), a, shifted(b, 4, 0))
+
+
+def pack_low(first, second):
+    sub = iota((8, 1024), 0)
+    a, b = [jnp.where(sub < 4, v[0:8], v[32:40]) for v in (first, second)]
+    return pack_pair(sub, a, b)
+
+
+def pack_high(first, second):
+    sub = iota((8, 1024), 0)
+    a, b = [jnp.where(sub >= 4, v[24:32], v[32:40]) for v in (first, second)]
+    return pack_pair(sub, a, b)
 
 
 def sides_kernel(pxl, pxh, vzl, vzh, out_l, out_h):
-    sub = iota((8, 1024), 0)
-    for ref, out, low_side in ((pxl, out_l, True), (pxh, out_h, False)):
-        out[...] = ref[...]
-        for message, start, f_plane in ((vzl, 0, 1), (vzh, 32, 2)):
-            planes = message[...].astype(F32).reshape(5, 40, 1024)
-            for pair in range(2):
-                added = []
-                for i in (2 * pair, 2 * pair + 1):
-                    v, f = planes[i], planes[4]
-                    f_low = shifted(f[0:8], 4, 0) if i == f_plane else 0.0
-                    f_high = shifted(f[24:32], 5, 0) if i == f_plane else 0.0
-                    if low_side:
-                        added.append(pack_low(sub, v[0:8], v[32:40], f_low))
-                    else:
-                        added.append(pack_high(sub, v[24:32], v[32:40], f_high))
-                rows = slice((start + 2 * pair) * 8, (start + 2 * pair) * 8 + 16)
-                total = ref[rows, :].astype(F32) + jnp.concatenate(added, axis=0)
-                out[rows, :] = total.astype(BF16)
-
-
-def merge_kernel(c1, r1, mzl, mzh, f1, q1, mxl, mxh):
+    out_l[...] = pxl[...]
+    out_h[...] = pxh[...]
+    for message, start in ((vzl, 0), (vzh, 128)):
+        planes = message[...].astype(F32).reshape(5, 40, 1024)
+        rows = slice(start, start + 16)
+        for ref, out, pack in ((pxl, out_l, pack_low), (pxh, out_h, pack_high)):
+            added = [pack(planes[2 * i], planes[2 * i + 1]) for i in range(2)]
+            out[rows, :] = (ref[rows, :].astype(F32) + jnp.concatenate(added, axis=0)).astype(BF16)
+
+
+def in_three(sub, tiles, free, turns):
+    spare = (sub == free) | (sub == free + 1)
+    last = tiles[:, 3]
+    parts = [jnp.where(spare, shifted(last, turn, 1), tiles[:, i]) for i, turn in enumerate(turns)]
+    return jnp.stack(parts, axis=1)
+
+
+def out_of_three(sub, parts, free, turns):
+    last = None
+    for i, turn in enumerate(turns):
+        back = shifted(parts[:, i], -turn, 1)
+        home = (free - turn) % 8
+        here = (sub == home) | (sub == home + 1)
+        last = jnp.where(here, back, 0.0 if last is None else last)
+    return jnp.stack([parts[:, 0], parts[:, 1], parts[:, 2], last], axis=1)
+
+
+HIGH_PACK = (2, (-2, 4, 2))
+LOW_PACK = (4, (-2, 4, 2))
+
+
+def merge_kernel(c1, mzl, mzh, f1, mxl, mxh):
     zeros = jnp.zeros((24, 512), F32)
     for p in (0, 1, 22, 23):
         f1[p] = zeros
     f1[2:22] = c1[...]
-    low = mzl[...].astype(F32).reshape(10, 24, 512)
-    high = mzh[...].astype(F32).reshape(10, 24, 512)
-    f1[0:6] = f1[0:6] + low[0:6]
-    f1[18:24] = f1[18:24] + high[0:6]
-    q1[0:4] = low[6:10]
-    q1[20:24] = high[6:10]
-    q1[4:20, 0:16, :] = r1[...]
-    q1[4:20, 16:24, :] = jnp.zeros((16, 8, 512), F32)
-    sub = iota((24, 8, 512), 1)
-    first, last, halo = f1[:, 0:8], f1[:, 8:16], f1[:, 16:24]
-    to_high = jnp.where(sub >= 4, last, jnp.where(sub < 2, halo, 0.0))
-    to_low = jnp.where(sub >= 6, halo, jnp.where(sub < 4, first, 0.0))
-    mxh[0:192, :] = to_high.reshape(192, 512).astype(BF16)
-    mxh[192:384, :] = q1[:, 8:16].reshape(192, 512).astype(BF16)
-    mxl[0:192, :] = to_low.reshape(192, 512).astype(BF16)
-    mxl[192:384, :] = q1[:, 0:8].reshape(192, 512).astype(BF16)
-
-
-def middle_kernel(nz, nx, info, f0, q0, mxl, mxh, f1, g1, v1, g2, va, rs, xp):
+    f1[0:6] = f1[0:6] + mzl[...].astype(F32).reshape(6, 24, 512)
+    f1[18:24] = f1[18:24] + mzh[...].astype(F32).reshape(6, 24, 512)
+    sub = iota((6, 8, 512), 1)
+    first, last, halo = [f1[:, 8 * n : 8 * n + 8].reshape(6, 4, 8, 512) for n in range(3)]
+    sub4 = iota((6, 4, 8, 512), 2)
+    to_high = in_three(sub, jnp.where(sub4 >= 4, last, halo), *HIGH_PACK)
+    to_low = in_three(sub, jnp.where(sub4 >= 4, halo, first), *LOW_PACK)
+    mxh[...] = to_high.reshape(144, 512).astype(BF16)
+    mxl[...] = to_low.reshape(144, 512).astype(BF16)
+
+
+def middle_kernel(nz, nx, info, f0, q_in, cl, ch, mxl, mxh, f1, g1, v1, g2, g2l, g2h, q0, va, rs, xp):
     iz, ix = info[0], info[1]
     k = spread(1)
     base = 1.0 + 6.0 * k
-    low = mxl[...].astype(F32).reshape(48, 8, 512)
-    high = mxh[...].astype(F32).reshape(48, 8, 512)
+    sub6 = iota((6, 8, 512), 1)
+    low = out_of_three(sub6, mxl[...].astype(F32).reshape(6, 3, 8, 512), *HIGH_PACK).reshape(24, 8, 512)
+    high = out_of_three(sub6, mxh[...].astype(F32).reshape(6, 3, 8, 512), *LOW_PACK).reshape(24, 8, 512)
     sub = iota((24, 8, 512), 1)
-    f1[:, 0:8] = f0[:, 0:8] + jnp.where(sub < 2, low[0:24], 0.0)
-    f1[:, 8:16] = f0[:, 8:16] + jnp.where(sub >= 6, high[0:24], 0.0)
-    f1[:, 16:24] = f0[:, 16:24] + jnp.where(sub >= 4, low[0:24], high[0:24])
-    q0[:, 16:24] = jnp.where(sub >= 4, low[24:48], high[24:48])
+    f1[:, 0:8] = f0[:, 0:8] + jnp.where(sub < 2, low, 0.0)
+    f1[:, 8:16] = f0[:, 8:16] + jnp.where(sub >= 6, high, 0.0)
+    f1[:, 16:24] = f0[:, 16:24] + jnp.where(sub >= 4, low, high)
+    low = cl[0:96, :].astype(F32).reshape(12, 8, 512)
+    high = ch[0:96, :].astype(F32).reshape(12, 8, 512)
+    sub12 = iota((12, 8, 512), 1)
+    even = jnp.where(sub12 >= 4, shifted(low, 4, 1), high)
+    odd = jnp.where(sub12 >= 4, low, shifted(high, 4, 1))
+    q0[:, 0:16] = q_in[:, 0:16]
+    q0[:, 16:24] = jnp.stack([even, odd], axis=1).reshape(24, 8, 512)
     shape = (24, 24, 128)
     valid = inside(shape, 0, -4, None, iz, 16, nz) & inside(shape, 1, 0, 20, ix, 16, nx)
     for t in range(4):
@@ -406,45 +544,34 @@
     loop(0, 8, coarse)
     for t, tile in enumerate(halve_lanes(xp, 8, 8)):
         g2[:, lanes(t)] = tile.reshape(64, 128)
+        g2l[:, lanes(t)] = tile[0:4].reshape(32, 128)
+        g2h[:, lanes(t)] = tile[4:8].reshape(32, 128)
 
 
 def back_kernel(
-    nz, nx, info, f1, g1, v1, vzl, vzh, vxl, vxh, g2, r2, v_in, g_in, s_in,
+    nz, nx, info, f1, g1, v1, vzl, vzh, vxl, vxh, own2, n2l, n2h, m2l, m2h, q_own, cl, ch, w2l, w2h, v_in, g_in, s_in,
     out,
     f2, q2, h2, a2, b2, rs, xp, xpr, wa, w1, zsl, zsh, vb, ws,
-    g2s, r2s, v2, gg, supply, sems, sems2,
+    v2, gg, supply, fsl, fsh, sems,
 ):
     iz, ix = info[0], info[1]
     matrix = doubling()
-
-    x_first = jnp.clip(ix - 2, 0, nx - 5)
-    near = []
-    for dz in range(5):
-        at = pl.ds(jnp.clip(iz + dz - 2, 0, nz - 1) * nx + x_first, 5)
-        near.append(pltpu.make_async_copy(g2.at[at], g2s.at[dz], sems2.at[0, dz]))
-        near.append(pltpu.make_async_copy(r2.at[at], r2s.at[dz], sems2.at[1, dz]))
     level0 = [
         pltpu.make_async_copy(src, dst, sems.at[i])
         for i, (src, dst) in enumerate(((v_in, v2), (g_in, gg), (s_in, supply)))
     ]
-    for copy in near + level0:
+    for copy in level0:
         copy.start()
-    for copy in near:
-        copy.wait()
-
-    sub4 = iota((8, 8, 256), 1)
-    for dz in range(-2, 3):
-        lo = 4 if dz == -2 else 0
-        hi = 4 if dz == 2 else 8
-        planes = slice(12 + 8 * dz + lo, 12 + 8 * dz + hi)
-        for src, ref in ((g2s, f2), (r2s, q2)):
-            parts = {}
-            for dx in range(-2, 3):
-                at = jnp.clip(ix + dx, 0, nx - 1) - x_first
-                parts[dx] = src[dz + 2, at].reshape(8, 8, 256)
-            far = jnp.where(sub4 < 4, parts[2], parts[-2])
-            for n, tile in enumerate((parts[0], parts[1], far, parts[-1])):
-                ref[planes, 8 * n : 8 * n + 8, :] = tile[lo:hi]
+
+    f2[:, 0:8, :] = own2[...]
+    f2[:, 8:16, :] = n2h[...].astype(F32).reshape(32, 8, 256)
+    f2[:, 16:24, :] = far_tile(m2l[...].astype(F32), m2h[...].astype(F32))
+    f2[:, 24:32, :] = n2l[...].astype(F32).reshape(32, 8, 256)
+    q2[:, 0:8, :] = q_own[...]
+    q2[:, 16:24, :] = far_tile(w2l[...].astype(F32), w2h[...].astype(F32))
+    for ref, rows in ((ch, slice(8, 16)), (cl, slice(24, 32))):
+        q2[0:16, rows, :] = ref[96:224, 0:256].astype(F32).reshape(16, 8, 256)
+        q2[16:32, rows, :] = ref[96:224, 256:512].astype(F32).reshape(16, 8, 256)
 
     k = spread(2)
     base = 1.0 + 6.0 * k
@@ -557,41 +684,54 @@
 
     s8 = iota((8, 128), 0)
 
-    def correct(m):
-        rows = pl.ds(pl.multiple_of(16 * m, 16), 16)
+    outer = outer_rows(s8)
+
+    def correct(i):
+        rows = pl.ds(pl.multiple_of(16 * i, 16), 16)
         for t in range(NT):
-            part = ws[m, :, lanes(t)]
-            rs[t, pl.ds(0, 24, stride=2), :] = part
-            rs[t, pl.ds(1, 24, stride=2), :] = part
             low = vxl[rows, lanes(t)].astype(F32)
             high = vxh[rows, lanes(t)].astype(F32)
-            for j in range(2):
-                p = 2 * m + j
-                lo, hi = low[8 * j : 8 * j + 8], high[8 * j : 8 * j + 8]
-                v2[p, 0:8, lanes(t)] = v2[p, 0:8, lanes(t)] + rs[t, 0:8, :] + jnp.where(s8 < 2, lo, 0.0)
-                v2[p, 8:24, lanes(t)] = v2[p, 8:24, lanes(t)] + rs[t, 8:24, :]
-                v2[p, 24:32, lanes(t)] = v2[p, 24:32, lanes(t)] + rs[t, 24:32, :] + jnp.where(s8 >= 6, hi, 0.0)
-                extra = jnp.where(s8 >= 6, lo, jnp.where(s8 < 2, hi, 0.0))
-                v2[p, 32:40, lanes(t)] = v2[p, 32:40, lanes(t)] + rs[t, 32:40, :] + extra
-
-    loop(0, 18, correct)
+            for n in range(2):
+                part = ws[2 * i + n, :, lanes(t)]
+                rs[t, pl.ds(0, 24, stride=2), :] = part
+                rs[t, pl.ds(1, 24, stride=2), :] = part
+                for j in range(2):
+                    p = 4 * i + 2 * n + j
+                    lo, hi = low[8 * n : 8 * n + 8], high[8 * n : 8 * n + 8]
+                    if j:
+                        lo, hi = shifted(lo, 4, 0), shifted(hi, 4, 0)
+                    v2[p, 0:8, lanes(t)] = v2[p, 0:8, lanes(t)] + rs[t, 0:8, :] + jnp.where(s8 < 2, lo, 0.0)
+                    v2[p, 8:24, lanes(t)] = v2[p, 8:24, lanes(t)] + rs[t, 8:24, :]
+                    v2[p, 24:32, lanes(t)] = v2[p, 24:32, lanes(t)] + rs[t, 24:32, :] + jnp.where(s8 >= 6, hi, 0.0)
+                    extra = jnp.where(outer, jnp.where(s8 >= 4, lo, hi), 0.0)
+                    v2[p, 32:40, lanes(t)] = v2[p, 32:40, lanes(t)] + rs[t, 32:40, :] + extra
+
+    loop(0, 9, correct)
     k0 = spread(0)
 
     def first(i):
-        rows = pl.ds(pl.multiple_of(16 * i + 16, 16), 16)
-        for j in range(2):
-            z = 2 * i + j
+        rows = pl.ds(pl.multiple_of(16 * i + 144, 16), 16)
+        for t in range(NT):
+            fsl[:, lanes(t)] = vxl[rows, lanes(t)].astype(F32)
+            fsh[:, lanes(t)] = vxh[rows, lanes(t)].astype(F32)
+
+        def step(j):
+            z = 16 * i + j
+            start = pl.multiple_of((j // 8) * 8, 8)
+            turn = lax.rem(j, 8)
             here, sums = plane(v2, z + 2)
             for t in range(NT):
-                lo = vxl[rows, lanes(t)].astype(F32)[8 * j : 8 * j + 8]
-                hi = vxh[rows, lanes(t)].astype(F32)[8 * j : 8 * j + 8]
-                f = jnp.where(s8 == 7, shifted(lo, 3, 0), jnp.where(s8 == 0, shifted(hi, 4, 0), 0.0))
+                lo = pltpu.roll(fsl[pl.ds(start, 8), lanes(t)], 7 - turn, 0)
+                hi = pltpu.roll(fsh[pl.ds(start, 8), lanes(t)], lax.rem(8 - turn, 8), 0)
+                f = jnp.where(s8 == 7, lo, jnp.where(s8 == 0, hi, 0.0))
                 g = gg[z + 2, :, lanes(t)]
                 inner = k0 * sums[t]
                 vb[z + 1, 0:32, lanes(t)] = KEEP * here[t][0:32] + g[0:32] * (supply[z, :, lanes(t)] + inner[0:32])
                 vb[z + 1, 32:40, lanes(t)] = KEEP * here[t][32:40] + g[32:40] * (f + inner[32:40])
 
-    loop(0, 16, first)
+        loop(0, 16, step)
+
+    loop(0, 2, first)
     for p, ref in ((1, zsl), (34, zsh)):
         here, sums = plane(v2, p)
         for t in range(NT):
@@ -629,9 +769,9 @@
     return jax.ShapeDtypeStruct(shape, dtype)
 
 
-def both_ways(to_low, to_high, axis):
+def both_ways(to_low, to_high, axis, distance=1):
     count = lax.axis_size(axis)
-    up = [(i, i + 1) for i in range(count - 1)]
+    up = [(i, i + distance) for i in range(count - distance)]
     down = [(j, i) for i, j in up]
     return lax.ppermute(to_high, axis, up), lax.ppermute(to_low, axis, down)
 
@@ -640,42 +780,52 @@
     nz, nx = lax.axis_size("gz"), lax.axis_size("xy")
     info = jnp.stack([lax.axis_index("gz"), lax.axis_index("xy")]).astype(jnp.int32)
     scratch = pltpu.VMEM
+    half = lambda *shape: shaped(shape, BF16)
+    full = lambda *shape: shaped(shape, F32)
 
     (blocks,) = call(
         lambda *refs: brick_kernel(2 * nx, *refs),
-        [shaped((9, 272, 128), BF16)],
+        [half(9, 272, 128)],
         [scratch((SLOTS, BRICK), F32)],
         2,
         (brick_ids, slot_counts, brick_values),
     )
-    uzl, uzh = both_ways(uptake[0:2].astype(BF16), uptake[30:32].astype(BF16), "gz")
     zl, zh = both_ways(blocks[0:3], blocks[6:9], "gz")
-    r1, r2 = call(
+    r1, r2, rzl, rzh, rz2l, rz2h, uxl, uxh = call(
         rates_kernel,
-        [shaped((16, 16, 512)), shaped((64, 256))],
+        [full(16, 16, 512), full(64, 256), half(128, 1024), half(128, 1024), half(32, 256), half(32, 256), half(64, 1024), half(64, 1024)],
         [scratch((8, 32, 128), F32), scratch((8, 16, 16, 128), F32), scratch((4, 16, 128), F32), scratch((4, 8, 8, 128), F32)],
         0,
         (uptake,),
     )
-    r2_all = lax.all_gather(r2, ("gz", "xy"))
-    column = lambda s: jnp.concatenate([uzl[:, s].astype(F32), uptake[:, s], uzh[:, s].astype(F32)], axis=0)
-    uxl, uxr = both_ways(column(slice(0, 2)), column(slice(30, 32)), "xy")
+    rzl, rzh = both_ways(rzl, rzh, "gz")
+    rz2l, rz2h = both_ways(rz2l, rz2h, "gz", 2)
     hop = lambda d: jnp.stack([blocks[3 + d], zl[d], zh[d]])
     xl, xr = both_ways(hop(0), hop(2), "xy")
+    q1, q2, ul, uh, cl, ch, wl, wh = call(
+        rates_window_kernel,
+        [full(24, 24, 512), full(32, 8, 256), half(80, 1024), half(80, 1024), half(224, 512), half(224, 512), half(128, 256), half(128, 256)],
+        [],
+        0,
+        (r1, r2, uxl, uxh, rzl, rzh, rz2l, rz2h),
+    )
+    ul, uh = both_ways(ul, uh, "xy")
+    cl, ch = both_ways(cl, ch, "xy")
+    wl, wh = both_ways(wl, wh, "xy", 2)
 
     supply, c1, mzl, mzh, vzl, vzh, pxl, pxh, v2, gg = call(
         lambda *refs: pre_kernel(nz, nx, *refs),
         [
-            shaped((C, C, 1024)),
-            shaped((20, 24, 512)),
-            shaped((240, 512), BF16),
-            shaped((240, 512), BF16),
-            shaped((200, 1024), BF16),
-            shaped((200, 1024), BF16),
-            shaped((288, 1024), BF16),
-            shaped((288, 1024), BF16),
-            shaped((36, 40, 1024)),
-            shaped((36, 40, 1024)),
+            full(C, C, 1024),
+            full(20, 24, 512),
+            half(144, 512),
+            half(144, 512),
+            half(200, 1024),
+            half(200, 1024),
+            half(176, 1024),
+            half(176, 1024),
+            full(36, 40, 1024),
+            full(36, 40, 1024),
         ],
         [
             scratch((42, 40, 1024), F32),
@@ -685,43 +835,56 @@
             scratch((1024, 1152), BF16),
             scratch((8, 40, 128), F32),
             scratch((8, 20, 24, 128), F32),
+            scratch((80, 1024), F32),
+            scratch((80, 1024), F32),
             pltpu.SemaphoreType.DMA((2,)),
         ],
         1,
-        (info, density, uptake, uzl, uzh, uxl, uxr, blocks, zl, zh, xl, xr, r1),
+        (info, density, uptake, rzl, rzh, ul, uh, blocks, zl, zh, xl, xr),
         [VMEM] * 8 + [ANY] * 2,
     )
     mzl, mzh = both_ways(mzl, mzh, "gz")
     vzl, vzh = both_ways(vzl, vzh, "gz")
-    f1, q1, mxl, mxh = call(
+    f1, mxl, mxh = call(
         merge_kernel,
-        [shaped((24, 24, 512)), shaped((24, 24, 512)), shaped((384, 512), BF16), shaped((384, 512), BF16)],
+        [full(24, 24, 512), half(144, 512), half(144, 512)],
         [],
         0,
-        (c1, r1, mzl, mzh),
+        (c1, mzl, mzh),
     )
     mxl, mxh = both_ways(mxl, mxh, "xy")
     pxl, pxh = call(
         sides_kernel,
-        [shaped((288, 1024), BF16), shaped((288, 1024), BF16)],
+        [half(176, 1024), half(176, 1024)],
         [],
         0,
         (pxl, pxh, vzl, vzh),
     )
-    f1, g1, v1, g2 = call(
+    vxl, vxh = both_ways(pxl, pxh, "xy")
+    f1, pxl, pxh = lax.optimization_barrier((f1, pxl, pxh))
+    f1, g1, v1, g2, g2l, g2h = call(
         lambda *refs: middle_kernel(nz, nx, *refs),
-        [shaped((24, 24, 512)), shaped((24, 24, 512)), shaped((24, 24, 512)), shaped((64, 256))],
-        [scratch((24, 24, 512), F32), scratch((4, 16, 128), F32), scratch((4, 8, 8, 128), F32)],
+        [full(24, 24, 512), full(24, 24, 512), full(24, 24, 512), full(64, 256), full(32, 256), full(32, 256)],
+        [scratch((24, 24, 512), F32), scratch((24, 24, 512), F32), scratch((4, 16, 128), F32), scratch((4, 8, 8, 128), F32)],
         1,
-        (info, f1, q1, mxl, mxh),
+        (info, f1, q1, cl, ch, mxl, mxh),
     )
-    g2_all = lax.all_gather(g2, ("gz", "xy"))
-    vxl, vxh = both_ways(pxl, pxh, "xy")
+    low, high = both_ways(g2, g2, "gz")
+    low2, high2 = both_ways(g2l, g2h, "gz", 2)
+    own2, near, fl, fh = call(
+        source_window_kernel,
+        [full(32, 8, 256), half(256, 256), half(128, 256), half(128, 256)],
+        [],
+        0,
+        (g2, low, high, low2, high2),
+    )
+    nl, nh = both_ways(near, near, "xy")
+    fl, fh = both_ways(fl, fh, "xy", 2)
     window2 = scratch((32, 32, 256), F32)
     window1 = scratch((24, 24, 512), F32)
     (concentration,) = call(
         lambda *refs: back_kernel(nz, nx, *refs),
-        [shaped((C, C, 1024))],
+        [full(C, C, 1024)],
         [
             window2, window2, window2, window2, window2,
             scratch((8, 48, 128), F32),
@@ -732,17 +895,16 @@
             scratch((200, 1024), F32),
             scratch((34, 40, 1024), F32),
             scratch((18, 24, 1024), F32),
-            scratch((5, 5, 64, 256), F32),
-            scratch((5, 5, 64, 256), F32),
             scratch((36, 40, 1024), F32),
             scratch((36, 40, 1024), F32),
             scratch((C, C, 1024), F32),
+            scratch((16, 1024), F32),
+            scratch((16, 1024), F32),
             pltpu.SemaphoreType.DMA((3,)),
-            pltpu.SemaphoreType.DMA((2, 5)),
         ],
         1,
-        (info, f1, g1, v1, vzl, vzh, vxl, vxh, g2_all, r2_all, v2, gg, supply),
-        in_hbm=5,
+        (info, f1, g1, v1, vzl, vzh, vxl, vxh, own2, nl, nh, fl, fh, q2, cl, ch, wl, wh, v2, gg, supply),
+        in_hbm=3,
     )
     return supply, concentration
 

time: 240 us -> 199 us (0.83)
  waiting for transfers between devices: 79.5 us -> 22.2 us
  starting transfers between devices: 46.7 us -> 79.8 us
  between operations: 14.4 us -> 1.54 us
  other arithmetic: 3.55 us -> 0.65 us
    ppermute x16 -> x30, starting transfers between devices: 46.6 us -> 79.8 us  [both_ways(): return (lax.ppermute(to_high, axis, up), lax.ppermute(to_low, axis, down))]
    ppermute x16 -> x30, waiting for transfers between devices: 52.1 us -> 22.2 us  [both_ways(): return (lax.ppermute(to_high, axis, up), lax.ppermute(to_low, axis, down))]
    all_gather x2 -> x0, waiting for transfers between devices: 27.4 us -> none  [the longest x1 27.4 us: shards(): g2_all = lax.all_gather(g2, ('gz', 'xy'))]
    another operation x1 -> x0, other arithmetic: 2.55 us -> none
    unnamed x36 -> x68, local copies, waits for them, and re-layouts: 3.17 us -> 5.2 us
    pallas_call x7 -> x9, Pallas kernels: 87.7 us -> 86.8 us  [call(): pl.pallas_call(kernel, out_shape=tuple(outs), in_specs=[SMEM] * smem + [V...]
  transfers between devices with their start and end apart: 18 -> 30, of which waited for: 7 -> 8; matrix products, arithmetic and copies ran while one was open for 3% -> 1% of each run, Pallas kernels for 21% -> 11%
where the time goes in v2:
time: 199 us; the launch traced here: 198 us
  Pallas kernels  86.8 us (44%)
  starting transfers between devices  79.8 us (40%)
  waiting for transfers between devices  22.2 us (11%)
  local copies, waits for them, and re-layouts  7.21 us (4%)
    pallas_call x9, Pallas kernels, call(): pl.pallas_call(kernel, out_shape=tuple(outs), in_specs=[SMEM] * smem + [V...  86.8 us
    ppermute x30, starting transfers between devices, both_ways(): return (lax.ppermute(to_high, axis, up), lax.ppermute(to_low, axis, down))  79.8 us
    ppermute x30, waiting for transfers between devices, both_ways(): return (lax.ppermute(to_high, axis, up), lax.ppermute(to_low, axis, down))  22.2 us
    unnamed x68, local copies, waits for them, and re-layouts  5.2 us
  transfers between devices with their start and end apart: 30, of which 8 were waited for; matrix products, arithmetic and copies ran while one was open for 1% of the time, Pallas kernels for 11%

profile of v2, /device:TPU:0, one launch (start us, length us, event | category | flops | bytes accessed | tf_op | source)
XLA Modules:
  0.0 198.2 jit_solution(1784167157662922886)
XLA Ops:
  0.6 4.5 %shard_map.70.refs_7_ = bf16[9,272,128]{2,1,0:T(8,128)(2,1)} custom-call(s32[72]{0:T(128)} %refs_0_.1, s32[1,9]{1,0:T(1,128)} %refs_1_.2, bf16[72,4096]{1,0:T(8,128)(2,1)} %refs_2_.2), custom_call_target="tpu_custom_call" | custom-call | flops 24336720 | bytes 1216836 | tf_op jit(solution)/shard_map/pallas_call | solution.py:757
  7.5 3.0 %collective-permute-start.6 = (bf16[3,272,128]{2,1,0:T(8,128)(2,1)S(1)}, bf16[3,272,128]{2,1,0:T(8,128)(2,1)S(1)}, u32[]{:S(2)}, u32[]{:S(2)}) collective-permute-start(bf16[3,272,128]{2,1,0:T(8,128)(2,1)S(1)} %get-tuple-element.89), channel_id=1, source_target_pairs={{0,8},{8,16},{16,24},{1,9},{9,17},{17,25},{2,10},{10,18},{18,26},{... | collective-permute-start | bytes 626696 | tf_op jit(solution)/shard_map/ppermute | solution.py:776
  10.6 4.6 %shard_map.68 = (f32[16,16,512]{2,1,0:T(8,128)}, f32[64,256]{1,0:T(8,128)}, bf16[128,1024]{1,0:T(8,128)(2,1)}, bf16[128,1024]{1,0:T(8,128)(2,1)}, bf16[32,256]{1...) custom-call(f32[32,32,1024]{2,1,0:T(8,128)} %refs_2_.3), custom_call_target="tpu_custom_call" | custom-call | flops 112066560 | bytes 5603328 | tf_op jit(solution)/shard_map/pallas_call | solution.py:757
  15.2 4.5 %collective-permute-start = (bf16[128,1024]{1,0:T(8,128)(2,1)}, bf16[128,1024]{1,0:T(8,128)(2,1)S(1)}, u32[]{:S(2)}, u32[]{:S(2)}) collective-permute-start(bf16[128,1024]{1,0:T(8,128)(2,1)} %get-tuple-element.44), channel_id=1, source_target_pairs={{0,8},{8,16},{16,24},{1,9},{9,17},{17,25},{2,10},{10,18},{18,26},{... | collective-permute-start | bytes 786440 | tf_op jit(solution)/shard_map/ppermute | solution.py:776
  19.7 1.3 collective-permute-start.1
  22.0 3.4 %collective-permute-start.8 = (bf16[3,272,128]{2,1,0:T(8,128)(2,1)S(1)}, bf16[3,272,128]{2,1,0:T(8,128)(2,1)S(1)}, u32[]{:S(2)}, u32[]{:S(2)}) collective-permute-start(bf16[3,272,128]{2,1,0:T(8,128)(2,1)S(1)} %pad_maximum_fusion), channel_id=1, source_target_pairs={{0,1},{1,2},{2,3},{3,4},{4,5},{5,6},{6,7},{8,9},{9,10},{10,11},{11... | collective-permute-start | bytes 626696 | tf_op jit(solution)/shard_map/ppermute | solution.py:776
  26.8 4.6 %collective-permute-start.2 = (bf16[32,256]{1,0:T(8,128)(2,1)}, bf16[32,256]{1,0:T(8,128)(2,1)S(1)}, u32[]{:S(2)}, u32[]{:S(2)}) collective-permute-start(bf16[32,256]{1,0:T(8,128)(2,1)} %get-tuple-element.50), channel_id=1, source_target_pairs={{0,16},{8,24},{1,17},{9,25},{2,18},{10,26},{3,19},{11,27},{4,20},{... | collective-permute-start | bytes 49160 | tf_op jit(solution)/shard_map/ppermute | solution.py:776
  31.4 1.6 collective-permute-done.2.z2l
  34.3 4.5 %collective-permute-done.3.z2h = bf16[32,256]{1,0:T(8,128)(2,1)S(1)} collective-permute-done((bf16[32,256]{1,0:T(8,128)(2,1)}, bf16[32,256]{1,0:T(8,128)(2,1)S(1)}, u32[]{:S(2)}, u32[]{:S(2)}) %collective-permute-start.3) | collective-permute-done | bytes 16416 | tf_op jit(solution)/shard_map/ppermute | solution.py:776
  39.7 2.8 %shard_map.69 = (f32[24,24,512]{2,1,0:T(8,128)}, f32[32,8,256]{2,1,0:T(8,128)}, bf16[80,1024]{1,0:T(8,128)(2,1)}, bf16[80,1024]{1,0:T(8,128)(2,1)}, bf16[224,512...) custom-call(f32[16,16,512]{2,1,0:T(8,128)} %get-tuple-element.46.r1, ...), custom_call_target="tpu_custom_call" | custom-call | flops 75366400 | bytes 3768320 | tf_op jit(solution)/shard_map/pallas_call | solution.py:757
  42.5 4.5 %collective-permute-start.4 = (bf16[80,1024]{1,0:T(8,128)(2,1)}, bf16[80,1024]{1,0:T(8,128)(2,1)S(1)}, u32[]{:S(2)}, u32[]{:S(2)}) collective-permute-start(bf16[80,1024]{1,0:T(8,128)(2,1)} %get-tuple-element.52), channel_id=1, source_target_pairs={{0,1},{1,2},{2,3},{3,4},{4,5},{5,6},{6,7},{8,9},{9,10},{10,11},{11... | collective-permute-start | bytes 491528 | tf_op jit(solution)/shard_map/ppermute | solution.py:776
  49.0 2.9 %collective-permute-done.4.refs_5_ = bf16[80,1024]{1,0:T(8,128)(2,1)S(1)} collective-permute-done((bf16[80,1024]{1,0:T(8,128)(2,1)}, bf16[80,1024]{1,0:T(8,128)(2,1)S(1)}, u32[]{:S(2)}, u32[]{:S(2)}) %collective-permute-start.4) | collective-permute-done | bytes 163872 | tf_op jit(solution)/shard_map/ppermute | solution.py:776
  51.9 3.0 %collective-permute-done.5.refs_6_ = bf16[80,1024]{1,0:T(8,128)(2,1)S(1)} collective-permute-done((bf16[80,1024]{1,0:T(8,128)(2,1)}, bf16[80,1024]{1,0:T(8,128)(2,1)S(1)}, u32[]{:S(2)}, u32[]{:S(2)}) %collective-permute-start.5) | collective-permute-done | bytes 163872 | tf_op jit(solution)/shard_map/ppermute | solution.py:776
  55.6 30.8 %shard_map.71 = (f32[32,32,1024]{2,1,0:T(8,128)}, f32[20,24,512]{2,1,0:T(8,128)}, bf16[144,512]{1,0:T(8,128)(2,1)}, bf16[144,512]{1,0:T(8,128)(2,1)}, bf16[200,1...) custom-call(s32[2]{0:T(128)} %pad_add_fusion.refs_0_, ...), custom_call_target="tpu_custom_call" | custom-call | flops 590233728 | bytes 29511688 | tf_op jit(solution)/shard_map/pallas_call | solution.py:757
  86.4 1.4 collective-permute-start.12
  89.2 3.0 %collective-permute-start.10 = (bf16[144,512]{1,0:T(8,128)(2,1)}, bf16[144,512]{1,0:T(8,128)(2,1)S(1)}, u32[]{:S(2)}, u32[]{:S(2)}) collective-permute-start(bf16[144,512]{1,0:T(8,128)(2,1)} %get-tuple-element.56), channel_id=1, source_target_pairs={{0,8},{8,16},{16,24},{1,9},{9,17},{17,25},{2,10},{10,18},{18,26},{... | collective-permute-start | bytes 442376 | tf_op jit(solution)/shard_map/ppermute | solution.py:776
  92.2 4.8 %collective-permute-start.14 = (bf16[224,512]{1,0:T(8,128)(2,1)S(1)}, bf16[224,512]{1,0:T(8,128)(2,1)S(1)}, u32[]{:S(2)}, u32[]{:S(2)}) collective-permute-start(bf16[224,512]{1,0:T(8,128)(2,1)S(1)} %copy-done.31), channel_id=1, source_target_pairs={{0,1},{1,2},{2,3},{3,4},{4,5},{5,6},{6,7},{8,9},{9,10},{10,11},{11... | collective-permute-start | bytes 688136 | tf_op jit(solution)/shard_map/ppermute | solution.py:776
  99.7 1.7 collective-permute-done.11.mzh
  102.1 2.5 %shard_map.72 = (f32[24,24,512]{2,1,0:T(8,128)}, bf16[144,512]{1,0:T(8,128)(2,1)}, bf16[144,512]{1,0:T(8,128)(2,1)}) custom-call(f32[20,24,512]{2,1,0:T(8,128)} %get-tuple-element.55.c1, bf16[144,512]{1,0:T(8,128)(2,1)} %copy-done.16, bf16[144,512]{1,0:T(8,128)(2,1)} %copy-done.17), custom_call_target="tpu_custom_call" | custom-call | flops 55050240 | bytes 2752512 | tf_op jit(solution)/shard_map/pallas_call | solution.py:757
  104.6 2.8 %collective-permute-start.16 = (bf16[144,512]{1,0:T(8,128)(2,1)}, bf16[144,512]{1,0:T(8,128)(2,1)S(1)}, u32[]{:S(2)}, u32[]{:S(2)}) collective-permute-start(bf16[144,512]{1,0:T(8,128)(2,1)} %get-tuple-element.69), channel_id=1, source_target_pairs={{0,1},{1,2},{2,3},{3,4},{4,5},{5,6},{6,7},{8,9},{9,10},{10,11},{11... | collective-permute-start | bytes 442376 | tf_op jit(solution)/shard_map/ppermute | solution.py:776
  109.5 2.3 %shard_map.73 = (bf16[176,1024]{1,0:T(8,128)(2,1)}, bf16[176,1024]{1,0:T(8,128)(2,1)}) custom-call(bf16[176,1024]{1,0:T(8,128)(2,1)} %get-tuple-element.59.pxl, bf16[176,1024]{1,0:T(8,128)(2,1)} %get-tuple-element.60.pxh, bf16[200,1024]{1,0:T(8,128)(2,1)} %copy-done, bf16[200,1024]{1,0:T(8,128)(2,1)} %copy-done.1), custom_call_target="tpu_custom_call" | custom-call | flops 45219840 | bytes 2260992 | tf_op jit(solution)/shard_map/pallas_call | solution.py:757
  113.2 5.3 %collective-permute-start.18 = (bf16[176,1024]{1,0:T(8,128)(2,1)}, bf16[176,1024]{1,0:T(8,128)(2,1)S(1)}, u32[]{:S(2)}, u32[]{:S(2)}) collective-permute-start(bf16[176,1024]{1,0:T(8,128)(2,1)} %get-tuple-element.64), channel_id=1, source_target_pairs={{0,1},{1,2},{2,3},{3,4},{4,5},{5,6},{6,7},{8,9},{9,10},{10,11},{11... | collective-permute-start | bytes 1081352 | tf_op jit(solution)/shard_map/ppermute | solution.py:776
  119.3 7.5 %shard_map.74 = (f32[24,24,512]{2,1,0:T(8,128)}, f32[24,24,512]{2,1,0:T(8,128)}, f32[24,24,512]{2,1,0:T(8,128)}, f32[64,256]{1,0:T(8,128)}, f32[32,256]{1,0:T(8,128)}, /*index=5*/f32[32,256]{1,0:T(8,128)}) custom-call(s32[2]{0:T(128)} %pad_add_fusion.refs_0_, f32[24,24,512]{2,1,0:T(8,128)} %get-tuple-element.65.refs_1_, ...), custom_call_target="tpu_custom_call" | custom-call | flops 135659680 | bytes 6782984 | tf_op jit(solution)/shard_map/pallas_call | solution.py:757
  128.1 7.6 %collective-permute-start.22 = (f32[32,256]{1,0:T(8,128)}, f32[32,256]{1,0:T(8,128)S(1)}, u32[]{:S(2)}, u32[]{:S(2)}) collective-permute-start(f32[32,256]{1,0:T(8,128)} %get-tuple-element.75), channel_id=1, source_target_pairs={{0,16},{8,24},{1,17},{9,25},{2,18},{10,26},{3,19},{11,27},{4,20},{... | collective-permute-start | bytes 98312 | tf_op jit(solution)/shard_map/ppermute | solution.py:776
  138.9 2.8 %collective-permute-done.23.high2 = f32[32,256]{1,0:T(8,128)S(1)} collective-permute-done((f32[32,256]{1,0:T(8,128)}, f32[32,256]{1,0:T(8,128)S(1)}, u32[]{:S(2)}, u32[]{:S(2)}) %collective-permute-start.23) | collective-permute-done | bytes 32800 | tf_op jit(solution)/shard_map/ppermute | solution.py:776
  141.7 4.8 %collective-permute-start.28 = (bf16[128,256]{1,0:T(8,128)(2,1)S(1)}, bf16[128,256]{1,0:T(8,128)(2,1)S(1)}, u32[]{:S(2)}, u32[]{:S(2)}) collective-permute-start(bf16[128,256]{1,0:T(8,128)(2,1)S(1)} %copy-done.33), channel_id=1, source_target_pairs={{0,2},{1,3},{2,4},{3,5},{4,6},{5,7},{8,10},{9,11},{10,12},{11,13},... | collective-permute-start | bytes 196616 | tf_op jit(solution)/shard_map/ppermute | solution.py:776
  148.5 1.7 shard_map.75
  150.2 4.5 %collective-permute-start.26 = (bf16[128,256]{1,0:T(8,128)(2,1)}, bf16[128,256]{1,0:T(8,128)(2,1)S(1)}, u32[]{:S(2)}, u32[]{:S(2)}) collective-permute-start(bf16[128,256]{1,0:T(8,128)(2,1)} %get-tuple-element.79), channel_id=1, source_target_pairs={{0,2},{1,3},{2,4},{3,5},{4,6},{5,7},{8,10},{9,11},{10,12},{11,13},... | collective-permute-start | bytes 196616 | tf_op jit(solution)/shard_map/ppermute | solution.py:776
  156.1 4.6 %collective-permute-start.24 = (bf16[256,256]{1,0:T(8,128)(2,1)}, bf16[256,256]{1,0:T(8,128)(2,1)S(1)}, u32[]{:S(2)}, u32[]{:S(2)}) collective-permute-start(bf16[256,256]{1,0:T(8,128)(2,1)} %get-tuple-element.78), channel_id=1, source_target_pairs={{0,1},{1,2},{2,3},{3,4},{4,5},{5,6},{6,7},{8,9},{9,10},{10,11},{11... | collective-permute-start | bytes 393224 | tf_op jit(solution)/shard_map/ppermute | solution.py:776
  160.7 1.5 collective-permute-start.27
  162.2 4.9 %collective-permute-done.27.refs_12_ = bf16[128,256]{1,0:T(8,128)(2,1)S(1)} collective-permute-done((bf16[128,256]{1,0:T(8,128)(2,1)}, bf16[128,256]{1,0:T(8,128)(2,1)S(1)}, u32[]{:S(2)}, u32[]{:S(2)}) %collective-permute-start.27) | collective-permute-done | bytes 65568 | tf_op jit(solution)/shard_map/ppermute | solution.py:776
  168.1 30.0 %shard_map.76 = f32[32,32,1024]{2,1,0:T(8,128)} custom-call(s32[2]{0:T(128)} %pad_add_fusion.refs_0_, f32[24,24,512]{2,1,0:T(8,128)} %get-tuple-element.71.refs_1_, f32[24,24,512]{2,1,0:T(8,128)} %get-tuple-element.72.refs_2_, f32[24,24,512]{2,1,0:T(8,128)} %get-tuple-element.73.refs_3_, bf16[200,1024]{1,0:T(8,128)(2,1)} %copy-done, ...), custom_call_target="tpu_custom_call" | custom-call | flops 535429280 | bytes 26771464 | tf_op jit(solution)/shard_map/pallas_call | solution.py:757
  (112 shorter events, 26.5 us)
Async XLA Ops:
  6.2 15.7 %collective-permute-start.7 = (bf16[3,272,128]{2,1,0:T(8,128)(2,1)S(1)}, bf16[3,272,128]{2,1,0:T(8,128)(2,1)S(1)}, u32[]{:S(2)}, u32[]{:S(2)}) collective-permute-start(bf16[3,272,128]{2,1,0:T(8,128)(2,1)S(1)} %get-tuple-element.88), channel_id=1, source_target_pairs={{8,0},{16,8},{24,16},{9,1},{17,9},{25,17},{10,2},{18,10},{26,18},{... | collective-permute-start | bytes 626696 | tf_op jit(solution)/shard_map/ppermute | solution.py:776
  7.5 14.4 %collective-permute-start.6 = (bf16[3,272,128]{2,1,0:T(8,128)(2,1)S(1)}, bf16[3,272,128]{2,1,0:T(8,128)(2,1)S(1)}, u32[]{:S(2)}, u32[]{:S(2)}) collective-permute-start(bf16[3,272,128]{2,1,0:T(8,128)(2,1)S(1)} %get-tuple-element.89), channel_id=1, source_target_pairs={{0,8},{8,16},{16,24},{1,9},{9,17},{17,25},{2,10},{10,18},{18,26},{... | collective-permute-start | bytes 626696 | tf_op jit(solution)/shard_map/ppermute | solution.py:776
  15.2 23.7 %collective-permute-start = (bf16[128,1024]{1,0:T(8,128)(2,1)}, bf16[128,1024]{1,0:T(8,128)(2,1)S(1)}, u32[]{:S(2)}, u32[]{:S(2)}) collective-permute-start(bf16[128,1024]{1,0:T(8,128)(2,1)} %get-tuple-element.44), channel_id=1, source_target_pairs={{0,8},{8,16},{16,24},{1,9},{9,17},{17,25},{2,10},{10,18},{18,26},{... | collective-permute-start | bytes 786440 | tf_op jit(solution)/shard_map/ppermute | solution.py:776
  19.7 19.2 %collective-permute-start.1 = (bf16[128,1024]{1,0:T(8,128)(2,1)}, bf16[128,1024]{1,0:T(8,128)(2,1)S(1)}, u32[]{:S(2)}, u32[]{:S(2)}) collective-permute-start(bf16[128,1024]{1,0:T(8,128)(2,1)} %get-tuple-element.45), channel_id=1, source_target_pairs={{8,0},{16,8},{24,16},{9,1},{17,9},{25,17},{10,2},{18,10},{26,18},{... | collective-permute-start | bytes 786440 | tf_op jit(solution)/shard_map/ppermute | solution.py:776
  22.0 26.9 %collective-permute-start.8 = (bf16[3,272,128]{2,1,0:T(8,128)(2,1)S(1)}, bf16[3,272,128]{2,1,0:T(8,128)(2,1)S(1)}, u32[]{:S(2)}, u32[]{:S(2)}) collective-permute-start(bf16[3,272,128]{2,1,0:T(8,128)(2,1)S(1)} %pad_maximum_fusion), channel_id=1, source_target_pairs={{0,1},{1,2},{2,3},{3,4},{4,5},{5,6},{6,7},{8,9},{9,10},{10,11},{11... | collective-permute-start | bytes 626696 | tf_op jit(solution)/shard_map/ppermute | solution.py:776
  25.5 23.5 %collective-permute-start.9 = (bf16[3,272,128]{2,1,0:T(8,128)(2,1)S(1)}, bf16[3,272,128]{2,1,0:T(8,128)(2,1)S(1)}, u32[]{:S(2)}, u32[]{:S(2)}) collective-permute-start(bf16[3,272,128]{2,1,0:T(8,128)(2,1)S(1)} %pad_maximum_fusion.1), channel_id=1, source_target_pairs={{1,0},{2,1},{3,2},{4,3},{5,4},{6,5},{7,6},{9,8},{10,9},{11,10},{12... | collective-permute-start | bytes 626696 | tf_op jit(solution)/shard_map/ppermute | solution.py:776
  26.8 6.3 %collective-permute-start.2 = (bf16[32,256]{1,0:T(8,128)(2,1)}, bf16[32,256]{1,0:T(8,128)(2,1)S(1)}, u32[]{:S(2)}, u32[]{:S(2)}) collective-permute-start(bf16[32,256]{1,0:T(8,128)(2,1)} %get-tuple-element.50), channel_id=1, source_target_pairs={{0,16},{8,24},{1,17},{9,25},{2,18},{10,26},{3,19},{11,27},{4,20},{... | collective-permute-start | bytes 49160 | tf_op jit(solution)/shard_map/ppermute | solution.py:776
  33.0 5.8 %collective-permute-start.3 = (bf16[32,256]{1,0:T(8,128)(2,1)}, bf16[32,256]{1,0:T(8,128)(2,1)S(1)}, u32[]{:S(2)}, u32[]{:S(2)}) collective-permute-start(bf16[32,256]{1,0:T(8,128)(2,1)} %get-tuple-element.51), channel_id=1, source_target_pairs={{16,0},{24,8},{17,1},{25,9},{18,2},{26,10},{19,3},{27,11},{20,4},{... | collective-permute-start | bytes 49160 | tf_op jit(solution)/shard_map/ppermute | solution.py:776
  42.5 9.4 %collective-permute-start.4 = (bf16[80,1024]{1,0:T(8,128)(2,1)}, bf16[80,1024]{1,0:T(8,128)(2,1)S(1)}, u32[]{:S(2)}, u32[]{:S(2)}) collective-permute-start(bf16[80,1024]{1,0:T(8,128)(2,1)} %get-tuple-element.52), channel_id=1, source_target_pairs={{0,1},{1,2},{2,3},{3,4},{4,5},{5,6},{6,7},{8,9},{9,10},{10,11},{11... | collective-permute-start | bytes 491528 | tf_op jit(solution)/shard_map/ppermute | solution.py:776
  47.0 7.8 %collective-permute-start.5 = (bf16[80,1024]{1,0:T(8,128)(2,1)}, bf16[80,1024]{1,0:T(8,128)(2,1)S(1)}, u32[]{:S(2)}, u32[]{:S(2)}) collective-permute-start(bf16[80,1024]{1,0:T(8,128)(2,1)} %get-tuple-element.53), channel_id=1, source_target_pairs={{1,0},{2,1},{3,2},{4,3},{5,4},{6,5},{7,6},{9,8},{10,9},{11,10},{12... | collective-permute-start | bytes 491528 | tf_op jit(solution)/shard_map/ppermute | solution.py:776
  86.4 55.3 %copy-start.33 = (bf16[128,256]{1,0:T(8,128)(2,1)S(1)}, bf16[128,256]{1,0:T(8,128)(2,1)}, u32[]{:S(2)}) copy-start(bf16[128,256]{1,0:T(8,128)(2,1)} %get-tuple-element.82) | copy-start | bytes 196612
  86.4 60.1 %copy-start.32 = (bf16[128,256]{1,0:T(8,128)(2,1)S(1)}, bf16[128,256]{1,0:T(8,128)(2,1)}, u32[]{:S(2)}) copy-start(bf16[128,256]{1,0:T(8,128)(2,1)} %get-tuple-element.83) | copy-start | bytes 196612
  86.4 21.0 %collective-permute-start.12 = (bf16[200,1024]{1,0:T(8,128)(2,1)}, bf16[200,1024]{1,0:T(8,128)(2,1)S(1)}, u32[]{:S(2)}, u32[]{:S(2)}) collective-permute-start(bf16[200,1024]{1,0:T(8,128)(2,1)} %get-tuple-element.61), channel_id=1, source_target_pairs={{0,8},{8,16},{16,24},{1,9},{9,17},{17,25},{2,10},{10,18},{18,26},{... | collective-permute-start | bytes 1228808 | tf_op jit(solution)/shard_map/ppermute | solution.py:776
  87.9 20.9 %collective-permute-start.13 = (bf16[200,1024]{1,0:T(8,128)(2,1)}, bf16[200,1024]{1,0:T(8,128)(2,1)S(1)}, u32[]{:S(2)}, u32[]{:S(2)}) collective-permute-start(bf16[200,1024]{1,0:T(8,128)(2,1)} %get-tuple-element.62), channel_id=1, source_target_pairs={{8,0},{16,8},{24,16},{9,1},{17,9},{25,17},{10,2},{18,10},{26,18},{... | collective-permute-start | bytes 1228808 | tf_op jit(solution)/shard_map/ppermute | solution.py:776
  89.2 9.2 %collective-permute-start.10 = (bf16[144,512]{1,0:T(8,128)(2,1)}, bf16[144,512]{1,0:T(8,128)(2,1)S(1)}, u32[]{:S(2)}, u32[]{:S(2)}) collective-permute-start(bf16[144,512]{1,0:T(8,128)(2,1)} %get-tuple-element.56), channel_id=1, source_target_pairs={{0,8},{8,16},{16,24},{1,9},{9,17},{17,25},{2,10},{10,18},{18,26},{... | collective-permute-start | bytes 442376 | tf_op jit(solution)/shard_map/ppermute | solution.py:776
  92.2 20.9 %collective-permute-start.14 = (bf16[224,512]{1,0:T(8,128)(2,1)S(1)}, bf16[224,512]{1,0:T(8,128)(2,1)S(1)}, u32[]{:S(2)}, u32[]{:S(2)}) collective-permute-start(bf16[224,512]{1,0:T(8,128)(2,1)S(1)} %copy-done.31), channel_id=1, source_target_pairs={{0,1},{1,2},{2,3},{3,4},{4,5},{5,6},{6,7},{8,9},{9,10},{10,11},{11... | collective-permute-start | bytes 688136 | tf_op jit(solution)/shard_map/ppermute | solution.py:776
  97.1 4.4 %collective-permute-start.11 = (bf16[144,512]{1,0:T(8,128)(2,1)}, bf16[144,512]{1,0:T(8,128)(2,1)S(1)}, u32[]{:S(2)}, u32[]{:S(2)}) collective-permute-start(bf16[144,512]{1,0:T(8,128)(2,1)} %get-tuple-element.57), channel_id=1, source_target_pairs={{8,0},{16,8},{24,16},{9,1},{17,9},{25,17},{10,2},{18,10},{26,18},{... | collective-permute-start | bytes 442376 | tf_op jit(solution)/shard_map/ppermute | solution.py:776
  98.4 20.1 %collective-permute-start.15 = (bf16[224,512]{1,0:T(8,128)(2,1)S(1)}, bf16[224,512]{1,0:T(8,128)(2,1)S(1)}, u32[]{:S(2)}, u32[]{:S(2)}) collective-permute-start(bf16[224,512]{1,0:T(8,128)(2,1)S(1)} %copy-done.30), channel_id=1, source_target_pairs={{1,0},{2,1},{3,2},{4,3},{5,4},{6,5},{7,6},{9,8},{10,9},{11,10},{12... | collective-permute-start | bytes 688136 | tf_op jit(solution)/shard_map/ppermute | solution.py:776
  104.6 13.9 %collective-permute-start.16 = (bf16[144,512]{1,0:T(8,128)(2,1)}, bf16[144,512]{1,0:T(8,128)(2,1)S(1)}, u32[]{:S(2)}, u32[]{:S(2)}) collective-permute-start(bf16[144,512]{1,0:T(8,128)(2,1)} %get-tuple-element.69), channel_id=1, source_target_pairs={{0,1},{1,2},{2,3},{3,4},{4,5},{5,6},{6,7},{8,9},{9,10},{10,11},{11... | collective-permute-start | bytes 442376 | tf_op jit(solution)/shard_map/ppermute | solution.py:776
  107.5 11.0 %collective-permute-start.17 = (bf16[144,512]{1,0:T(8,128)(2,1)}, bf16[144,512]{1,0:T(8,128)(2,1)S(1)}, u32[]{:S(2)}, u32[]{:S(2)}) collective-permute-start(bf16[144,512]{1,0:T(8,128)(2,1)} %get-tuple-element.70), channel_id=1, source_target_pairs={{1,0},{2,1},{3,2},{4,3},{5,4},{6,5},{7,6},{9,8},{10,9},{11,10},{12... | collective-permute-start | bytes 442376 | tf_op jit(solution)/shard_map/ppermute | solution.py:776
  111.9 55.2 %collective-permute-start.19 = (bf16[176,1024]{1,0:T(8,128)(2,1)}, bf16[176,1024]{1,0:T(8,128)(2,1)S(1)}, u32[]{:S(2)}, u32[]{:S(2)}) collective-permute-start(bf16[176,1024]{1,0:T(8,128)(2,1)} %get-tuple-element.63), channel_id=1, source_target_pairs={{1,0},{2,1},{3,2},{4,3},{5,4},{6,5},{7,6},{9,8},{10,9},{11,10},{12... | collective-permute-start | bytes 1081352 | tf_op jit(solution)/shard_map/ppermute | solution.py:776
  113.2 53.9 %collective-permute-start.18 = (bf16[176,1024]{1,0:T(8,128)(2,1)}, bf16[176,1024]{1,0:T(8,128)(2,1)S(1)}, u32[]{:S(2)}, u32[]{:S(2)}) collective-permute-start(bf16[176,1024]{1,0:T(8,128)(2,1)} %get-tuple-element.64), channel_id=1, source_target_pairs={{0,1},{1,2},{2,3},{3,4},{4,5},{5,6},{6,7},{8,9},{9,10},{10,11},{11... | collective-permute-start | bytes 1081352 | tf_op jit(solution)/shard_map/ppermute | solution.py:776
  126.8 19.7 %collective-permute-start.21 = (f32[64,256]{1,0:T(8,128)}, f32[64,256]{1,0:T(8,128)S(1)}, u32[]{:S(2)}, u32[]{:S(2)}) collective-permute-start(f32[64,256]{1,0:T(8,128)} %get-tuple-element.74.own), channel_id=1, source_target_pairs={{8,0},{16,8},{24,16},{9,1},{17,9},{25,17},{10,2},{18,10},{26,18},{... | collective-permute-start | bytes 196616 | tf_op jit(solution)/shard_map/ppermute | solution.py:776
  128.1 9.5 %collective-permute-start.22 = (f32[32,256]{1,0:T(8,128)}, f32[32,256]{1,0:T(8,128)S(1)}, u32[]{:S(2)}, u32[]{:S(2)}) collective-permute-start(f32[32,256]{1,0:T(8,128)} %get-tuple-element.75), channel_id=1, source_target_pairs={{0,16},{8,24},{1,17},{9,25},{2,18},{10,26},{3,19},{11,27},{4,20},{... | collective-permute-start | bytes 98312 | tf_op jit(solution)/shard_map/ppermute | solution.py:776
  135.7 6.0 %collective-permute-start.23 = (f32[32,256]{1,0:T(8,128)}, f32[32,256]{1,0:T(8,128)S(1)}, u32[]{:S(2)}, u32[]{:S(2)}) collective-permute-start(f32[32,256]{1,0:T(8,128)} %get-tuple-element.76), channel_id=1, source_target_pairs={{16,0},{24,8},{17,1},{25,9},{18,2},{26,10},{19,3},{27,11},{20,4},{... | collective-permute-start | bytes 98312 | tf_op jit(solution)/shard_map/ppermute | solution.py:776
  137.6 10.2 %collective-permute-start.20 = (f32[64,256]{1,0:T(8,128)}, f32[64,256]{1,0:T(8,128)S(1)}, u32[]{:S(2)}, u32[]{:S(2)}) collective-permute-start(f32[64,256]{1,0:T(8,128)} %get-tuple-element.74.own), channel_id=1, source_target_pairs={{0,8},{8,16},{16,24},{1,9},{9,17},{17,25},{2,10},{10,18},{18,26},{... | collective-permute-start | bytes 196616 | tf_op jit(solution)/shard_map/ppermute | solution.py:776
  141.7 13.1 %collective-permute-start.28 = (bf16[128,256]{1,0:T(8,128)(2,1)S(1)}, bf16[128,256]{1,0:T(8,128)(2,1)S(1)}, u32[]{:S(2)}, u32[]{:S(2)}) collective-permute-start(bf16[128,256]{1,0:T(8,128)(2,1)S(1)} %copy-done.33), channel_id=1, source_target_pairs={{0,2},{1,3},{2,4},{3,5},{4,6},{5,7},{8,10},{9,11},{10,12},{11,13},... | collective-permute-start | bytes 196616 | tf_op jit(solution)/shard_map/ppermute | solution.py:776
  146.5 9.6 %collective-permute-start.29 = (bf16[128,256]{1,0:T(8,128)(2,1)S(1)}, bf16[128,256]{1,0:T(8,128)(2,1)S(1)}, u32[]{:S(2)}, u32[]{:S(2)}) collective-permute-start(bf16[128,256]{1,0:T(8,128)(2,1)S(1)} %copy-done.32), channel_id=1, source_target_pairs={{2,0},{3,1},{4,2},{5,3},{6,4},{7,5},{10,8},{11,9},{12,10},{13,11},... | collective-permute-start | bytes 196616 | tf_op jit(solution)/shard_map/ppermute | solution.py:776
  150.2 10.4 %collective-permute-start.26 = (bf16[128,256]{1,0:T(8,128)(2,1)}, bf16[128,256]{1,0:T(8,128)(2,1)S(1)}, u32[]{:S(2)}, u32[]{:S(2)}) collective-permute-start(bf16[128,256]{1,0:T(8,128)(2,1)} %get-tuple-element.79), channel_id=1, source_target_pairs={{0,2},{1,3},{2,4},{3,5},{4,6},{5,7},{8,10},{9,11},{10,12},{11,13},... | collective-permute-start | bytes 196616 | tf_op jit(solution)/shard_map/ppermute | solution.py:776
  154.8 12.3 %collective-permute-start.25 = (bf16[256,256]{1,0:T(8,128)(2,1)}, bf16[256,256]{1,0:T(8,128)(2,1)S(1)}, u32[]{:S(2)}, u32[]{:S(2)}) collective-permute-start(bf16[256,256]{1,0:T(8,128)(2,1)} %get-tuple-element.78), channel_id=1, source_target_pairs={{1,0},{2,1},{3,2},{4,3},{5,4},{6,5},{7,6},{9,8},{10,9},{11,10},{12... | collective-permute-start | bytes 393224 | tf_op jit(solution)/shard_map/ppermute | solution.py:776
  156.1 11.0 %collective-permute-start.24 = (bf16[256,256]{1,0:T(8,128)(2,1)}, bf16[256,256]{1,0:T(8,128)(2,1)S(1)}, u32[]{:S(2)}, u32[]{:S(2)}) collective-permute-start(bf16[256,256]{1,0:T(8,128)(2,1)} %get-tuple-element.78), channel_id=1, source_target_pairs={{0,1},{1,2},{2,3},{3,4},{4,5},{5,6},{6,7},{8,9},{9,10},{10,11},{11... | collective-permute-start | bytes 393224 | tf_op jit(solution)/shard_map/ppermute | solution.py:776
  160.7 6.4 %collective-permute-start.27 = (bf16[128,256]{1,0:T(8,128)(2,1)}, bf16[128,256]{1,0:T(8,128)(2,1)S(1)}, u32[]{:S(2)}, u32[]{:S(2)}) collective-permute-start(bf16[128,256]{1,0:T(8,128)(2,1)} %get-tuple-element.80), channel_id=1, source_target_pairs={{2,0},{3,1},{4,2},{5,3},{6,4},{7,5},{10,8},{11,9},{12,10},{13,11},... | collective-permute-start | bytes 196616 | tf_op jit(solution)/shard_map/ppermute | solution.py:776
  (32 other events, 247.6 us)
